TPU v7x, 768 devices: a whole 4x8x12 slice. The times are simulated.
768 devices in a mesh: dp: 384 (over x_hi, z, y, core), opt: 2 (over x_lo).
Axes of the slice: x: 4 (x_hi: 2, x_lo: 2; x = x_hi * 2 + x_lo), y: 8, z: 12, core: 2. Of those that a mesh axis runs over, the one named last changes fastest.
Arguments:
- img_resid: bfloat16 [98304, 1152], P(('dp', 'opt')), may hold values from -6 to 6
- img_hidden: bfloat16 [98304, 1024], P(('dp', 'opt')), may hold values from -6 to 6
- txt_resid: bfloat16 [98304, 1152], P('dp'), may hold values from -6 to 6
- txt_hidden: bfloat16 [98304, 1024], P('dp'), may hold values from -6 to 6
- edge_weight: bfloat16 [2, 1024, 128], replicated, may hold values from -0.1875 to 0.1875
- left_root: float32 [2, 1024, 1024], P('opt'), may hold values from -0.125 to 2
- right_root: float32 [2, 128, 128], P('opt'), may hold values from -0.35355339 to 2
- graft_acc: float32 [2, 1024, 128], P('opt'), may hold values from 1e-07 to 100
Outputs:
- updates: float32 [2, 1024, 128], P('opt')
All inputs are finite; a program needn't handle non-finite values.
Results may differ from a plain program's by a relative error of at most 0.0038.
Values may be sent and summed in bfloat16 or wider, within the bound.
A program may use at most 32 MiB of HBM per device.

v0:
```python
import jax
import jax.numpy as jnp
from jax import lax
from jax.sharding import PartitionSpec as P

WINDOW = 3


def shifted(block, axis, distance):
    devices = range(lax.axis_size(axis))
    route = [((i - distance) % len(devices), i) for i in devices]
    return lax.ppermute(block, axis, route)


def embed_rows(resid, hidden, weight, split_at):
    edge_part = jnp.dot(hidden, weight, preferred_element_type=jnp.float32)
    stream = resid.astype(jnp.float32)
    stream = jnp.concatenate([stream[:, :split_at], stream[:, split_at:] + edge_part], axis=1)
    length = jnp.sqrt(jnp.sum(stream * stream, axis=1, keepdims=True) + 1e-06)
    return (stream / length, length)


def back_norm(direction, length, grads, split_at):
    radial = jnp.sum(direction * grads, axis=1, keepdims=True)
    return ((grads - direction * radial) / length)[:, split_at:].astype(jnp.bfloat16)


def pair_weights(left_emb, right_emb, left_start, right_start):
    logits = 10.0 * jnp.dot(left_emb, right_emb.T, preferred_element_type=jnp.float32) - 2.0
    row_ids = left_start + lax.broadcasted_iota(jnp.int32, logits.shape, 0)
    col_ids = right_start + lax.broadcasted_iota(jnp.int32, logits.shape, 1)
    return (jax.nn.sigmoid(logits) - (row_ids == col_ids).astype(jnp.float32)).astype(jnp.bfloat16)


def precondition(block_grad, left_mat, right_mat, accum):
    highest = lax.Precision.HIGHEST
    conditioned = jnp.dot(
        jnp.dot(left_mat, block_grad, precision=highest), right_mat, precision=highest
    )
    grafted = block_grad / jnp.sqrt(accum + block_grad * block_grad)
    factor = jnp.sqrt(jnp.sum(grafted * grafted)) / jnp.sqrt(
        jnp.sum(conditioned * conditioned) + 1e-06
    )
    return conditioned * factor


def on_device(
    img_resid, img_hidden, txt_resid, txt_hidden, edge_weight, left_root, right_root, graft_acc
):
    split_at = img_hidden.shape[1]
    dp_count = lax.axis_size("dp")
    opt_count = lax.axis_size("opt")
    dp_pos = lax.axis_index("dp")
    opt_pos = lax.axis_index("opt")
    img_count = img_resid.shape[0]
    txt_count = txt_resid.shape[0]
    features = img_resid.shape[1]
    img_dir, img_len = embed_rows(img_resid, img_hidden, edge_weight[0], split_at)
    txt_dir, txt_len = embed_rows(txt_resid, txt_hidden, edge_weight[1], split_at)
    img_emb = img_dir.astype(jnp.bfloat16)
    txt_emb = txt_dir.astype(jnp.bfloat16)
    img_start = (dp_pos * opt_count + opt_pos) * img_count
    img_grad = jnp.zeros((img_count, features), jnp.float32)
    txt_part = jnp.zeros((txt_count, features), jnp.float32)
    visiting = txt_emb
    for offset in range(WINDOW):
        source = (dp_pos - offset) % dp_count
        weights_bf = pair_weights(img_emb, visiting, img_start, source * txt_count)
        img_grad = img_grad + jnp.dot(weights_bf, visiting, preferred_element_type=jnp.float32)
        txt_part = txt_part + jnp.dot(weights_bf.T, img_emb, preferred_element_type=jnp.float32)
        if offset + 1 < WINDOW:
            visiting = shifted(visiting, "dp", 1)
            txt_part = shifted(txt_part, "dp", 1)
    txt_part = shifted(txt_part, "dp", 1 - WINDOW)
    img_dz = back_norm(img_dir, img_len, img_grad, split_at)
    row_start = opt_pos * img_count
    txt_rows = lax.dynamic_slice_in_dim(txt_hidden, row_start, img_count, 0)
    own_grad = lax.psum_scatter(txt_part, "opt", scatter_dimension=0, tiled=True)
    own_dir = lax.dynamic_slice_in_dim(txt_dir, row_start, img_count, 0)
    own_len = lax.dynamic_slice_in_dim(txt_len, row_start, img_count, 0)
    txt_dz_rows = back_norm(own_dir, own_len, own_grad, split_at)
    local_terms = jnp.stack(
        [
            jnp.dot(img_hidden.T, img_dz, preferred_element_type=jnp.float32),
            jnp.dot(txt_rows.T, txt_dz_rows, preferred_element_type=jnp.float32),
        ]
    )
    summed = lax.psum(local_terms, ("dp", "opt"))
    owned = lax.dynamic_index_in_dim(summed, opt_pos, 0, keepdims=True)
    result = precondition(owned[0], left_root[0], right_root[0], graft_acc[0])
    return result[None]


def solution(mesh):
    placed = (
        P(("dp", "opt"), None),
        P(("dp", "opt"), None),
        P("dp", None),
        P("dp", None),
        P(),
        P("opt", None, None),
        P("opt", None, None),
        P("opt", None, None),
    )
    return jax.shard_map(
        on_device, mesh=mesh, in_specs=placed, out_specs=P("opt", None, None), check_vma=False
    )
```

profile of v0, /device:TPU:1, one launch (start us, length us, event | category | flops | bytes accessed | tf_op | source)
XLA Modules:
  0.0 642.6 jit_solution(7416291526127222718)
XLA Ops:
  6.5 1.3 copy.18
  7.8 0.9 convert_element_type.32
  9.0 1.1 convert_element_type.34
  10.2 0.8 copy-done.3
  11.0 1.2 convolution_add_fusion.4
  12.5 0.9 fusion.50
  13.4 1.2 convolution_add_fusion.3
  14.8 1.0 fusion.48
  15.7 1.4 fusion.20
  17.2 1.3 fusion.53
  18.5 4.6 collective-permute-start.2
  23.2 1.9 collective-permute-start
  25.1 17.7 %collective-permute-done = bf16[256,1152]{0,1:T(8,128)(2,1)} collective-permute-done((bf16[256,1152]{0,1:T(8,128)(2,1)S(1)}, bf16[256,1152]{0,1:T(8,128)(2,1)}, u32[]{:S(2)}, u32[]{:S(2)}) %collective-permute-start) | collective-permute-done | bytes 589856 | tf_op jit(solution)/shard_map/ppermute | solution.py:12
  42.8 1.4 fusion.21
  44.2 2.6 convolution_add_fusion
  46.8 4.5 collective-permute-start.3
  51.3 1.9 collective-permute-start.1
  53.3 17.8 %collective-permute-done.1 = bf16[256,1152]{0,1:T(8,128)(2,1)} collective-permute-done((bf16[256,1152]{0,1:T(8,128)(2,1)}, bf16[256,1152]{0,1:T(8,128)(2,1)}, u32[]{:S(2)}, u32[]{:S(2)}) %collective-permute-start.1) | collective-permute-done | bytes 589856 | tf_op jit(solution)/shard_map/ppermute | solution.py:12
  71.1 1.4 fusion.22
  72.7 1.4 add.148
  74.2 23.5 %collective-permute-start.4 = (f32[256,1152]{0,1:T(8,128)S(1)}, f32[256,1152]{0,1:T(8,128)}, u32[]{:S(2)}, u32[]{:S(2)}) collective-permute-start(f32[256,1152]{0,1:T(8,128)S(1)} %add.148), channel_id=1, source_target_pairs={{4,0},{6,2},{8,4},{10,6},{12,8},{14,10},{16,12},{18,14},{20,16},{2... | collective-permute-start | bytes 3538952 | tf_op jit(solution)/shard_map/ppermute | solution.py:12
  97.7 24.4 %collective-permute-done.4 = f32[256,1152]{0,1:T(8,128)} collective-permute-done((f32[256,1152]{0,1:T(8,128)S(1)}, f32[256,1152]{0,1:T(8,128)}, u32[]{:S(2)}, u32[]{:S(2)}) %collective-permute-start.4) | collective-permute-done | bytes 1179680 | tf_op jit(solution)/shard_map/ppermute | solution.py:12
  122.6 1.4 convolution_add_fusion.2
  124.0 1.5 multiply_reduce_fusion.2
  125.7 23.5 %reduce-scatter.2.cloned.1.call-done = f32[128,1152]{0,1:T(8,128)} async-done(((f32[256,1152]{0,1:T(8,128)}), f32[128,1152]{0,1:T(8,128)}) %reduce-scatter.2.cloned.1.call-update) | async-done | bytes 589840 | tf_op jit(solution)/shard_map/reduce_scatter | solution.py:78
  149.2 1.2 multiply_reduce_fusion.1
  150.4 1.0 convolution_bitcast_fusion
  151.5 1.1 pad_maximum_fusion.1
  152.6 470.7 %all-reduce.2.cloned.1.call-done = f32[2,1024,128]{1,2,0:T(8,128)} async-done(((f32[2,1024,128]{1,2,0:T(8,128)}), f32[2,1024,128]{1,2,0:T(8,128)}) %all-reduce.2.cloned.1.call-update) | async-done | bytes 1048592 | tf_op jit(solution)/shard_map/psum | solution.py:88
  623.3 1.1 constant_dynamic-slice_fusion
  624.6 6.6 %fusion = f32[128,1024]{1,0:T(8,128)S(1)} fusion(f32[1,1024,1024]{2,1,0:T(8,128)} %param.13, f32[1,1024,128]{1,2,0:T(8,128)S(1)} %constant_dynamic-slice_fusion), kind=kOutput, calls=%fused_computation | convolution fusion | flops 1610612736 | bytes 5242880 | tf_op jit(solution)/shard_map/dot_general | solution.py:38
  631.2 1.6 multiply_reduce_fusion.4
  (39 shorter events, 3.5 us)
Async XLA Ops:
  6.5 6.8 %copy-start = (bf16[256,1024]{1,0:T(8,128)(2,1)S(1)}, bf16[256,1024]{1,0:T(8,128)(2,1)}, u32[]{:S(2)}) copy-start(bf16[256,1024]{1,0:T(8,128)(2,1)} %param.11) | copy-start | bytes 1572868
  6.5 142.7 %reduce-scatter.2.cloned.1.call-start = ((), (), s32[]{:S(2)}) async-start(), calls=%async_computation.1 | async-start | bytes 1769472 | tf_op jit(solution)/shard_map/reduce_scatter | solution.py:78
  6.5 2.2 copy-start.4
  10.1 0.9 copy-start.3
  12.3 1.1 copy-start.5
  15.7 7.4 %copy-start.2 = (bf16[256,1152]{0,1:T(8,128)(2,1)S(1)}, bf16[256,1152]{0,1:T(8,128)(2,1)}, u32[]{:S(2)}) copy-start(bf16[256,1152]{0,1:T(8,128)(2,1)} %get-tuple-element.5) | copy-start | bytes 1769476
  18.5 25.6 %collective-permute-start.2 = (f32[256,1152]{0,1:T(8,128)}, f32[256,1152]{0,1:T(8,128)}, u32[]{:S(2)}, u32[]{:S(2)}) collective-permute-start(f32[256,1152]{0,1:T(8,128)} %fusion.53), channel_id=1, source_target_pairs={{766,0},{0,2},{2,4},{4,6},{6,8},{8,10},{10,12},{12,14},{14,16},{16... | collective-permute-start | bytes 3538952 | tf_op jit(solution)/shard_map/ppermute | solution.py:12
  23.2 19.6 %collective-permute-start = (bf16[256,1152]{0,1:T(8,128)(2,1)S(1)}, bf16[256,1152]{0,1:T(8,128)(2,1)}, u32[]{:S(2)}, u32[]{:S(2)}) collective-permute-start(bf16[256,1152]{0,1:T(8,128)(2,1)S(1)} %copy-done.2), channel_id=1, source_target_pairs={{766,0},{0,2},{2,4},{4,6},{6,8},{8,10},{10,12},{12,14},{14,16},{16... | collective-permute-start | bytes 1769480 | tf_op jit(solution)/shard_map/ppermute | solution.py:12
  46.8 25.9 %collective-permute-start.3 = (f32[256,1152]{0,1:T(8,128)}, f32[256,1152]{0,1:T(8,128)}, u32[]{:S(2)}, u32[]{:S(2)}) collective-permute-start(f32[256,1152]{0,1:T(8,128)} %convolution_add_fusion), channel_id=1, source_target_pairs={{766,0},{0,2},{2,4},{4,6},{6,8},{8,10},{10,12},{12,14},{14,16},{16... | collective-permute-start | bytes 3538952 | tf_op jit(solution)/shard_map/ppermute | solution.py:12
  51.3 19.8 %collective-permute-start.1 = (bf16[256,1152]{0,1:T(8,128)(2,1)}, bf16[256,1152]{0,1:T(8,128)(2,1)}, u32[]{:S(2)}, u32[]{:S(2)}) collective-permute-start(bf16[256,1152]{0,1:T(8,128)(2,1)} %collective-permute-done), channel_id=1, source_target_pairs={{766,0},{0,2},{2,4},{4,6},{6,8},{8,10},{10,12},{12,14},{14,16},{16... | collective-permute-start | bytes 1769480 | tf_op jit(solution)/shard_map/ppermute | solution.py:12
  74.2 47.9 %collective-permute-start.4 = (f32[256,1152]{0,1:T(8,128)S(1)}, f32[256,1152]{0,1:T(8,128)}, u32[]{:S(2)}, u32[]{:S(2)}) collective-permute-start(f32[256,1152]{0,1:T(8,128)S(1)} %add.148), channel_id=1, source_target_pairs={{4,0},{6,2},{8,4},{10,6},{12,8},{14,10},{16,12},{18,14},{20,16},{2... | collective-permute-start | bytes 3538952 | tf_op jit(solution)/shard_map/ppermute | solution.py:12
  122.1 501.2 %all-reduce.2.cloned.1.call-start = ((), (), s32[]{:S(2)}) async-start(), calls=%async_computation.2 | async-start | bytes 2097152 | tf_op jit(solution)/shard_map/psum | solution.py:88
  122.6 1.5 copy-start.1
  624.6 6.6 %copy-start.7 = (f32[1,128,128]{2,1,0:T(8,128)S(1)}, f32[1,128,128]{2,1,0:T(8,128)}, u32[]{:S(2)}) copy-start(f32[1,128,128]{2,1,0:T(8,128)} %param.14) | copy-start | bytes 196612
  631.2 2.3 copy-start.6
Sparse Core Ops, SparseCore 0:
  122.3 26.8 reduce-scatter.1
  155.5 467.8 all-reduce.1
where the time goes:
time: 645 us; the launch traced here: 643 us
  waiting for transfers between devices  554 us (86%)
  starting transfers between devices  36.5 us (6%)
  matrix products  23.5 us (4%)
  between operations  15.1 us (2%)
  other arithmetic  9.59 us (1%)
    psum x1, waiting for transfers between devices, on_device(): summed = lax.psum(local_terms, ('dp', 'opt'))  471 us
    ppermute x5, waiting for transfers between devices, shifted(): return lax.ppermute(block, axis, route)  59.9 us
    ppermute x5, starting transfers between devices, shifted(): return lax.ppermute(block, axis, route)  36.5 us
    reduce_scatter x1, waiting for transfers between devices, on_device(): lax.psum_scatter(txt_part, 'opt', scatter_dimension=0, tiled=True)  23.5 us
  transfers between devices with their start and end apart: 7, of which 5 were waited for; matrix products, arithmetic and copies ran while one was open for 1% of the time, Pallas kernels for 0%

commit v1 on v0

v1 whole, which is shorter than its diff:
```python
import functools

import jax
import jax.numpy as jnp
from jax import lax
from jax.experimental import pallas as pl
from jax.experimental.pallas import tpu as pltpu
from jax.sharding import PartitionSpec as P

WINDOW = 3
NX, NY, NZ = 2, 8, 12
MESH = pl.DeviceIdType.MESH
F32 = jnp.float32
BF16 = jnp.bfloat16


def shifted(block, axis, distance):
    devices = range(lax.axis_size(axis))
    route = [((i - distance) % len(devices), i) for i in devices]
    return lax.ppermute(block, axis, route)


def embed_rows(resid, hidden, weight, split_at):
    edge_part = jnp.dot(hidden, weight, preferred_element_type=F32)
    stream = resid.astype(F32)
    stream = jnp.concatenate([stream[:, :split_at], stream[:, split_at:] + edge_part], axis=1)
    length = jnp.sqrt(jnp.sum(stream * stream, axis=1, keepdims=True) + 1e-06)
    return (stream / length, length)


def edge_back(direction, length, edge_grad, radial, split_at):
    return ((edge_grad - direction[:, split_at:] * radial) / length).astype(BF16)


class Place:
    def __init__(self):
        dp = lax.axis_index("dp")
        self.xl = lax.axis_index("opt")
        self.core = lax.rem(dp, 2)
        self.y = lax.rem(lax.div(dp, 2), NY)
        self.z = lax.rem(lax.div(dp, 2 * NY), NZ)
        self.xh = lax.div(dp, 2 * NY * NZ)

    def at(self, xh=None, z=None, y=None, core=None, xl=None):
        xh = self.xh if xh is None else xh
        z = self.z if z is None else z
        y = self.y if y is None else y
        core = self.core if core is None else core
        xl = self.xl if xl is None else xl
        return (((xh * NZ + z) * NY + y) * 2 + core, xl)


def reduce_kernel(
    p_ref, left_hbm, right_ref, acc_ref, out_ref,
    left_ref, cbuf, acc1, xsend, xbuf, acc2, ysend, ybuf, zbuf, gbuf, cond,
    load_sem, csend_sem, crecv_sem, xs_sem, xr_sem, ys_sem, yr_sem, zs_sem, zr_sem,
    gs_sem, gr_sem, hs_sem, hr_sem, ks_sem, kr_sem,
):
    me = Place()
    load = pltpu.make_async_copy(left_hbm, left_ref, load_sem)
    load.start()
    oc = 1 - me.core
    x = me.xh * 2 + me.xl
    xpeer = []
    for k in range(1, 4):
        px = lax.rem(x + k, 4)
        xpeer.append((px, me.at(xh=lax.div(px, 2), xl=lax.rem(px, 2))))
    ypeer = [(lax.rem(me.y + k, NY), me.at(y=lax.rem(me.y + k, NY))) for k in range(1, NY)]
    zpeer = [(lax.rem(me.z + k, NZ), me.at(z=lax.rem(me.z + k, NZ))) for k in range(1, NZ)]
    cpeer = me.at(core=oc)
    hpeer = me.at(xh=1 - me.xh)

    barrier = pltpu.get_barrier_semaphore()
    peers = [cpeer] + [d for _, d in xpeer + ypeer + zpeer]
    for d in peers:
        pl.semaphore_signal(barrier, inc=1, device_id=d, device_id_type=MESH)
    pl.semaphore_wait(barrier, len(peers))

    def remote(src, dst, s, r, d):
        return pltpu.make_async_remote_copy(
            src_ref=src, dst_ref=dst, send_sem=s, recv_sem=r, device_id=d, device_id_type=MESH
        )

    mine = pl.ds(pl.multiple_of(me.core * 512, 512), 512)
    theirs = pl.ds(pl.multiple_of(oc * 512, 512), 512)
    sent = []
    ccopies = []
    for t in range(2):
        c = remote(p_ref.at[t, theirs], cbuf.at[t], csend_sem.at[t], crecv_sem.at[t], cpeer)
        c.start()
        ccopies.append(c)
    for t in range(2):
        ccopies[t].wait_recv()
        acc1[t] = p_ref[t, mine] + cbuf[t]
    sent += ccopies
    xcopies = []
    for k in (2, 1, 3):
        px, d = xpeer[k - 1]
        rows = pl.ds(pl.multiple_of(lax.div(px, 2) * 256, 256), 256)
        xsend[k - 1] = acc1[lax.rem(px, 2), rows].astype(BF16)
        c = remote(xsend.at[k - 1], xbuf.at[k - 1], xs_sem.at[k - 1], xr_sem.at[k - 1], d)
        c.start()
        xcopies.append(c)
    total = acc1[me.xl, pl.ds(pl.multiple_of(me.xh * 256, 256), 256)]
    for c, k in zip(xcopies, (2, 1, 3)):
        c.wait_recv()
    for k in range(3):
        total = total + xbuf[k].astype(F32)
    acc2[...] = total
    sent += xcopies
    ysend[...] = total.astype(BF16)
    ycopies = []
    for k in (4, 3, 5, 2, 6, 1, 7):
        py, d = ypeer[k - 1]
        c = remote(
            ysend.at[pl.ds(pl.multiple_of(py * 32, 32), 32)], ybuf.at[k - 1],
            ys_sem.at[k - 1], yr_sem.at[k - 1], d,
        )
        c.start()
        ycopies.append(c)
    part = acc2[pl.ds(pl.multiple_of(me.y * 32, 32), 32)]
    for c in ycopies:
        c.wait_recv()
    for k in range(NY - 1):
        part = part + ybuf[k].astype(F32)
    sent += ycopies
    zbuf[me.z] = part.astype(BF16)
    zcopies = []
    for k in (6, 5, 7, 4, 8, 3, 9, 2, 10, 1, 11):
        pz, d = zpeer[k - 1]
        c = remote(zbuf.at[me.z], zbuf.at[me.z], zs_sem.at[k - 1], zr_sem.at[k - 1], d)
        c.start()
        zcopies.append((k, c))
    for k, c in zcopies:
        src = lax.rem(me.z + NZ - k, NZ)
        remote(zbuf.at[src], zbuf.at[src], zs_sem.at[k - 1], zr_sem.at[k - 1], cpeer).wait_recv()
        sent.append(c)
    part = zbuf[0].astype(F32)
    for k in range(1, NZ):
        part = part + zbuf[k].astype(F32)
    base = me.core * 512 + me.xh * 256
    own = pl.ds(pl.multiple_of(base + me.y * 32, 32), 32)
    gbuf[own] = part
    gcopies = []
    for k in (4, 3, 5, 2, 6, 1, 7):
        py, d = ypeer[k - 1]
        c = remote(gbuf.at[own], gbuf.at[own], gs_sem.at[k - 1], gr_sem.at[k - 1], d)
        c.start()
        sent.append(c)
    for k in (4, 3, 5, 2, 6, 1, 7):
        src = lax.rem(me.y + NY - k, NY)
        rows = pl.ds(pl.multiple_of(base + src * 32, 32), 32)
        remote(gbuf.at[rows], gbuf.at[rows], gs_sem.at[k - 1], gr_sem.at[k - 1], cpeer).wait_recv()
    own = pl.ds(pl.multiple_of(base, 256), 256)
    other = pl.ds(pl.multiple_of(me.core * 512 + (1 - me.xh) * 256, 256), 256)
    c = remote(gbuf.at[own], gbuf.at[own], hs_sem, hr_sem, hpeer)
    c.start()
    sent.append(c)
    c = remote(gbuf.at[own], gbuf.at[own], ks_sem.at[0], kr_sem.at[0], cpeer)
    c.start()
    sent.append(c)
    remote(gbuf.at[other], gbuf.at[other], hs_sem, hr_sem, hpeer).wait_recv()
    c = remote(gbuf.at[other], gbuf.at[other], ks_sem.at[1], kr_sem.at[1], cpeer)
    c.start()
    sent.append(c)
    for q, xh in ((0, me.xh), (1, 1 - me.xh)):
        rows = pl.ds(pl.multiple_of(oc * 512 + xh * 256, 256), 256)
        remote(gbuf.at[rows], gbuf.at[rows], ks_sem.at[q], kr_sem.at[q], cpeer).wait_recv()
    for c in sent:
        c.wait_send()
    load.wait()
    grad = gbuf[...]
    grafted = grad / jnp.sqrt(acc_ref[...] + grad * grad)
    gnorm = jnp.sum(grafted * grafted)
    highest = lax.Precision.HIGHEST
    right = right_ref[...]

    def body(i, tot):
        rows = pl.ds(pl.multiple_of(i * 256, 256), 256)
        v = jnp.dot(left_ref[rows], gbuf[...], precision=highest, preferred_element_type=F32)
        v = jnp.dot(v, right, precision=highest, preferred_element_type=F32)
        cond[rows] = v
        return tot + jnp.sum(v * v)

    cnorm = lax.fori_loop(0, 4, body, jnp.float32(0.0))
    factor = jnp.sqrt(gnorm) / jnp.sqrt(cnorm + 1e-06)
    out_ref[...] = cond[...] * factor


def reduce_and_step(terms, left, right, accum):
    dma = pltpu.SemaphoreType.DMA
    vm = pl.BlockSpec(memory_space=pltpu.VMEM)
    return pl.pallas_call(
        reduce_kernel,
        out_shape=jax.ShapeDtypeStruct((1024, 128), F32),
        in_specs=[vm, pl.BlockSpec(memory_space=pl.ANY), vm, vm],
        out_specs=vm,
        scratch_shapes=[
            pltpu.VMEM((1024, 1024), F32),
            pltpu.VMEM((2, 512, 128), F32),
            pltpu.VMEM((2, 512, 128), F32),
            pltpu.VMEM((3, 256, 128), BF16),
            pltpu.VMEM((3, 256, 128), BF16),
            pltpu.VMEM((256, 128), F32),
            pltpu.VMEM((256, 128), BF16),
            pltpu.VMEM((NY - 1, 32, 128), BF16),
            pltpu.VMEM((NZ, 32, 128), BF16),
            pltpu.VMEM((1024, 128), F32),
            pltpu.VMEM((1024, 128), F32),
            dma, dma((2,)), dma((2,)), dma((3,)), dma((3,)),
            dma((NY - 1,)), dma((NY - 1,)), dma((NZ - 1,)), dma((NZ - 1,)),
            dma((NY - 1,)), dma((NY - 1,)), dma, dma, dma((2,)), dma((2,)),
        ],
        compiler_params=pltpu.CompilerParams(
            collective_id=0, has_side_effects=True, vmem_limit_bytes=48 << 20
        ),
    )(terms, left, right, accum)


def on_device(
    img_resid, img_hidden, txt_resid, txt_hidden, edge_weight, left_root, right_root, graft_acc
):
    split_at = img_hidden.shape[1]
    opt_pos = lax.axis_index("opt")
    img_count = img_resid.shape[0]
    txt_count = txt_resid.shape[0]
    img_dir, img_len = embed_rows(img_resid, img_hidden, edge_weight[0], split_at)
    img_emb = img_dir.astype(BF16)
    visitors = [img_emb] + [shifted(img_emb, "dp", -c) for c in range(1, WINDOW)]
    txt_dir, txt_len = embed_rows(txt_resid, txt_hidden, edge_weight[1], split_at)
    txt_emb = txt_dir.astype(BF16)
    row_start = opt_pos * img_count
    eye = (
        row_start + lax.broadcasted_iota(jnp.int32, (img_count, txt_count), 0)
        == lax.broadcasted_iota(jnp.int32, (img_count, txt_count), 1)
    ).astype(F32)
    txt_part = jnp.zeros((txt_count, split_at // 8), F32)
    txt_rad = jnp.zeros((txt_count,), F32)
    img_part = jnp.zeros((img_count + 8, split_at // 8), F32)
    for c in range(WINDOW):
        sims = jnp.dot(visitors[c], txt_emb.T, preferred_element_type=F32)
        probs = jax.nn.sigmoid(10.0 * sims - 2.0)
        if c == 0:
            probs = probs - eye
        wts = probs.astype(BF16)
        ws = wts.astype(F32) * sims
        back = jnp.concatenate(
            [
                jnp.dot(wts, txt_emb[:, split_at:], preferred_element_type=F32),
                jnp.broadcast_to(jnp.sum(ws, axis=1)[None], (8, img_count)),
            ]
        )
        img_part = img_part + (shifted(back, "dp", c) if c else back)
        txt_part = txt_part + jnp.dot(
            wts.T, visitors[c][:, split_at:], preferred_element_type=F32
        )
        txt_rad = txt_rad + jnp.sum(ws, axis=0)
    img_dz = edge_back(
        img_dir, img_len, img_part[:img_count], img_part[img_count][:, None], split_at
    )
    other = (1 - opt_pos) * img_count
    away = jnp.concatenate(
        [
            lax.dynamic_slice_in_dim(txt_part, other, img_count, 0),
            jnp.broadcast_to(lax.dynamic_slice_in_dim(txt_rad, other, img_count, 0)[None], (8, img_count)),
        ]
    )
    came = lax.ppermute(away, "opt", [(0, 1), (1, 0)])
    txt_rows = lax.dynamic_slice_in_dim(txt_hidden, row_start, img_count, 0)
    own_grad = lax.dynamic_slice_in_dim(txt_part, row_start, img_count, 0) + came[:img_count]
    own_rad = lax.dynamic_slice_in_dim(txt_rad, row_start, img_count, 0) + came[img_count]
    own_dir = lax.dynamic_slice_in_dim(txt_dir, row_start, img_count, 0)
    own_len = lax.dynamic_slice_in_dim(txt_len, row_start, img_count, 0)
    txt_dz = edge_back(own_dir, own_len, own_grad, own_rad[:, None], split_at)
    terms = jnp.stack(
        [
            jnp.dot(img_hidden.T, img_dz, preferred_element_type=F32),
            jnp.dot(txt_rows.T, txt_dz, preferred_element_type=F32),
        ]
    )
    return reduce_and_step(terms, left_root[0], right_root[0], graft_acc[0])[None]


def solution(mesh):
    placed = (
        P(("dp", "opt"), None),
        P(("dp", "opt"), None),
        P("dp", None),
        P("dp", None),
        P(),
        P("opt", None, None),
        P("opt", None, None),
        P("opt", None, None),
    )
    return jax.shard_map(
        on_device, mesh=mesh, in_specs=placed, out_specs=P("opt", None, None), check_vma=False
    )
```

time: 645 us -> 98.9 us (0.15)
  waiting for transfers between devices: 554 us -> 10.2 us
  Pallas kernels: 0 us -> 41 us
  between operations: 15.1 us -> 0.33 us
  matrix products: 23.5 us -> 10.2 us
  other arithmetic: 9.59 us -> 1.89 us
    psum x1 -> x0, waiting for transfers between devices: 471 us -> none  [on_device(): summed = lax.psum(local_terms, ('dp', 'opt'))]
    ppermute x5 -> x4, waiting for transfers between devices: 59.9 us -> 10.2 us  [shifted(): return lax.ppermute(block, axis, route)]
    pallas_call x0 -> x1, Pallas kernels: none -> 41 us  [reduce_and_step(): pl.pallas_call(reduce_kernel, out_shape=jax.ShapeDtypeStruct((1024, 128),...]
    reduce_scatter x1 -> x0, waiting for transfers between devices: 23.5 us -> none  [on_device(): lax.psum_scatter(txt_part, 'opt', scatter_dimension=0, tiled=True)]
    dot_general x15 -> x13, matrix products: 23.5 us -> 10.2 us  [the longest x3 4.06 us: on_device(): sims = jnp.dot(visitors[c], txt_emb.T, preferred_element_type=F32)]
    ppermute x5 -> x4, starting transfers between devices: 36.5 us -> 28.3 us  [shifted(): return lax.ppermute(block, axis, route)]
  transfers between devices with their start and end apart: 7 -> 5, of which waited for: 5 -> 1; matrix products, arithmetic and copies ran while one was open for 1% -> 6% of each run, Pallas kernels for 0% -> 0%
where the time goes in v1:
time: 98.9 us; the launch traced here: 98.2 us
  Pallas kernels  41 us (41%)
  starting transfers between devices  30.5 us (31%)
  matrix products  10.2 us (10%)
  waiting for transfers between devices  10.2 us (10%)
  local copies, waits for them, and re-layouts  4.11 us (4%)
  other arithmetic  1.89 us (2%)
    pallas_call x1, Pallas kernels, reduce_and_step(): pl.pallas_call(reduce_kernel, out_shape=jax.ShapeDtypeStruct((1024, 128),...  41 us
    ppermute x4, starting transfers between devices, shifted(): return lax.ppermute(block, axis, route)  28.3 us
    ppermute x4, waiting for transfers between devices, shifted(): return lax.ppermute(block, axis, route)  10.2 us
    dot_general x3, matrix products, on_device(): sims = jnp.dot(visitors[c], txt_emb.T, preferred_element_type=F32)  4.06 us
    unnamed x17, local copies, waits for them, and re-layouts  3.29 us
    dot_general x3, matrix products, on_device(): jnp.dot(wts.T, visitors[c][:, split_at:], preferred_element_type=F32)  2.82 us
    ppermute x1, starting transfers between devices, on_device(): came = lax.ppermute(away, 'opt', [(0, 1), (1, 0)])  2.22 us
  transfers between devices with their start and end apart: 5, of which 1 were waited for; matrix products, arithmetic and copies ran while one was open for 6% of the time, Pallas kernels for 0%

profile of v1, /device:TPU:1, one launch (start us, length us, event | category | flops | bytes accessed | tf_op | source)
XLA Modules:
  0.0 98.2 jit_solution(12060027160379399780)
XLA Ops:
  0.0 1.3 %copy.18 = bf16[128,1152]{0,1:T(8,128)(2,1)S(1)} copy(bf16[128,1152]{1,0:T(8,128)(2,1)} %param.8) | data formatting | bytes 589824 | tf_op args[0]
  1.4 0.3 convolution_add_fusion.3
  1.7 0.2 multiply_reduce_fusion.1
  1.9 1.0 %fusion.39 = (bf16[128,1152]{0,1:T(8,128)(2,1)}, f32[128,1152]{0,1:T(8,128)}) fusion(f32[128]{0:T(128)S(1)} %add_sqrt_fusion.1, f32[128,128]{0,1:T(8,128)S(1)} %convolution_add_fusion.3, f32[128,1024]{0,1:T(8,128)S(1)} %slice.66), kind=kLoop, calls=%fused_computation.69 | loop fusion | flops 442368 | bytes 1475072 | tf_op jit(solution)/shard_map/convert_element_type | solution.py:228
  2.9 20.5 %collective-permute-start.2 = (bf16[128,1152]{0,1:T(8,128)(2,1)}, bf16[128,1152]{0,1:T(8,128)(2,1)}, u32[]{:S(2)}, u32[]{:S(2)}) collective-permute-start(bf16[128,1152]{0,1:T(8,128)(2,1)} %get-tuple-element.14), channel_id=1, source_target_pairs={{4,0},{6,2},{8,4},{10,6},{12,8},{14,10},{16,12},{18,14},{20,16},{2... | collective-permute-start | bytes 884744 | tf_op jit(solution)/shard_map/ppermute | solution.py:20
  23.4 2.9 %collective-permute-start = (bf16[128,1152]{0,1:T(8,128)(2,1)}, bf16[128,1152]{0,1:T(8,128)(2,1)}, u32[]{:S(2)}, u32[]{:S(2)}) collective-permute-start(bf16[128,1152]{0,1:T(8,128)(2,1)} %get-tuple-element.14), channel_id=1, source_target_pairs={{2,0},{4,2},{6,4},{8,6},{10,8},{12,10},{14,12},{16,14},{18,16},{20... | collective-permute-start | bytes 884744 | tf_op jit(solution)/shard_map/ppermute | solution.py:20
  26.2 0.2 copy.19
  26.5 0.1 convert_element_type.41
  26.7 1.3 %convolution_add_fusion = f32[256,128]{0,1:T(8,128)S(1)} fusion(bf16[256,1024]{1,0:T(8,128)(2,1)S(1)} %copy-done, bf16[2,1024,128]{2,1,0:T(8,128)(2,1)} %param.12, f32[256,1152]{0,1:T(8,128)S(1)} %convert_element_type.41), kind=kOutput, calls=%fused_computation.4 | convolution fusion | flops 67141632 | bytes 1048576 | tf_op jit(solution)/shard_map/dot_general | solution.py:24
  28.0 0.2 multiply_reduce_fusion
  28.1 0.1 fusion.37
  28.3 1.4 %fusion.9 = (f32[128]{0:T(128)S(1)}, f32[256]{0:T(256)S(1)}, bf16[128,256]{1,0:T(8,128)(2,1)S(1)}) fusion(s32[128]{0:T(128)S(1)} %iota_add_fusion, bf16[128,1152]{0,1:T(8,128)(2,1)} %get-tuple-element.14, bf16[256,1152]{0,1:T(8,128)(2,1)S(1)} %get-tuple-element.12), kind=kOutput, calls=%fused_computation.31 | convolution fusion | flops 75923072 | bytes 952320 | tf_op jit(solution)/shard_map/dot_general | solution.py:241
  29.7 0.1 fusion.24
  29.8 0.1 dynamic-slice.3
  29.9 0.9 fusion.30
  30.8 1.3 %fusion.13 = (f32[128]{0:T(128)S(1)}, f32[256]{0:T(256)S(1)}, f32[128,256]{1,0:T(8,128)S(1)}) fusion(bf16[128,1152]{0,1:T(8,128)(2,1)} %collective-permute-done.2, bf16[256,1152]{0,1:T(8,128)(2,1)S(1)} %get-tuple-element.12), kind=kOutput, calls=%fused_computation.35 | convolution fusion | flops 75824768 | bytes 1017344 | tf_op jit(solution)/shard_map/dot_general | solution.py:241
  32.2 0.2 fusion.20
  32.4 1.4 %fusion.11 = (f32[128]{0:T(128)S(1)}, f32[256]{0:T(256)S(1)}, f32[128,256]{1,0:T(8,128)S(1)}) fusion(bf16[128,1152]{0,1:T(8,128)(2,1)} %collective-permute-done, bf16[256,1152]{0,1:T(8,128)(2,1)S(1)} %get-tuple-element.12), kind=kOutput, calls=%fused_computation.33 | convolution fusion | flops 75824768 | bytes 1017344 | tf_op jit(solution)/shard_map/dot_general | solution.py:241
  33.7 0.2 fusion.22
  34.0 0.9 convolution_add_fusion.2
  34.9 1.0 convolution_add_fusion.1
  36.0 2.2 %collective-permute-start.4 = (f32[136,128]{0,1:T(8,128)S(1)}, f32[136,128]{0,1:T(8,128)S(1)}, u32[]{:S(2)}, u32[]{:S(2)}) collective-permute-start(f32[136,128]{0,1:T(8,128)S(1)} %pad_maximum_fusion.5), channel_id=1, source_target_pairs={{0,1},{1,0},{2,3},{3,2},{4,5},{5,4},{6,7},{7,6},{8,9},{9,8},{10,11... | collective-permute-start | bytes 208904 | tf_op jit(solution)/shard_map/ppermute | solution.py:268
  38.4 1.9 %collective-permute-start.3 = (f32[136,128]{0,1:T(8,128)S(1)}, f32[136,128]{0,1:T(8,128)S(1)}, u32[]{:S(2)}, u32[]{:S(2)}) collective-permute-start(f32[136,128]{0,1:T(8,128)S(1)} %pad_maximum_fusion.4), channel_id=1, source_target_pairs={{764,0},{766,2},{0,4},{2,6},{4,8},{6,10},{8,12},{10,14},{12,16},{1... | collective-permute-start | bytes 208904 | tf_op jit(solution)/shard_map/ppermute | solution.py:20
  40.4 3.0 %collective-permute-start.1 = (f32[136,128]{0,1:T(8,128)S(1)}, f32[136,128]{0,1:T(8,128)S(1)}, u32[]{:S(2)}, u32[]{:S(2)}) collective-permute-start(f32[136,128]{0,1:T(8,128)S(1)} %pad_maximum_fusion.3), channel_id=1, source_target_pairs={{766,0},{0,2},{2,4},{4,6},{6,8},{8,10},{10,12},{12,14},{14,16},{16... | collective-permute-start | bytes 208904 | tf_op jit(solution)/shard_map/ppermute | solution.py:20
  43.4 0.1 slice_reduce_fusion
  43.6 10.2 %collective-permute-done.3 = f32[136,128]{0,1:T(8,128)S(1)} collective-permute-done((f32[136,128]{0,1:T(8,128)S(1)}, f32[136,128]{0,1:T(8,128)S(1)}, u32[]{:S(2)}, u32[]{:S(2)}) %collective-permute-start.3) | collective-permute-done | bytes 69664 | tf_op jit(solution)/shard_map/ppermute | solution.py:20
  53.9 0.1 slice_reduce_fusion.1
  54.0 1.1 %convolution_bitcast_fusion.1 = f32[1,1024,128]{2,1,0:T(8,128)S(1)} fusion(bf16[128,1024]{1,0:T(8,128)(2,1)S(1)} %copy-done.4, f32[128,1152]{0,1:T(8,128)} %get-tuple-element.15, f32[136,128]{0,1:T(8,128)S(1)} %fusion.7, f32[128]{0:T(128)S(1)} %add_sqrt_fusion.1, f32[128]{0:T(128)S(1)} %slice_reduce_fusion.1), kind=kOutput, calls=%fused_computation.1 | convolution fusion | flops 33619968 | bytes 918528 | tf_op jit(solution)/shard_map/dot_general | solution.py:277
  55.1 0.3 convolution_bitcast_fusion
  55.5 0.9 copy-done.1
  56.4 41.0 %shard_map.82 = f32[1024,128]{1,0:T(8,128)S(1)} custom-call(f32[2,1024,128]{2,1,0:T(8,128)S(1)} %pad_maximum_fusion.1.p_ref, f32[1024,1024]{1,0:T(8,128)} %bitcast.30, f32[128,128]{1,0:T(8,128)S(1)} %bitcast.29, f32[1024,128]{1,0:T(8,128)S(1)} %bitcast.28), custom_call_target="tpu_custom_call" | custom-call | tf_op jit(solution)/shard_map/pallas_call | solution.py:193
  97.4 0.8 copy.35
  (36 shorter events, 0.9 us)
Async XLA Ops:
  0.0 26.7 %copy-start = (bf16[256,1024]{1,0:T(8,128)(2,1)S(1)}, bf16[256,1024]{1,0:T(8,128)(2,1)}, u32[]{:S(2)}) copy-start(bf16[256,1024]{1,0:T(8,128)(2,1)} %param.11) | copy-start | bytes 1572868
  0.0 1.4 %copy-start.6 = (bf16[2,1024,128]{2,1,0:T(8,128)(2,1)S(1)}, bf16[2,1024,128]{2,1,0:T(8,128)(2,1)}, u32[]{:S(2)}) copy-start(bf16[2,1024,128]{2,1,0:T(8,128)(2,1)} %param.12) | copy-start | bytes 1572868
  0.0 1.4 %copy-start.3 = (bf16[128,1024]{1,0:T(8,128)(2,1)S(1)}, bf16[128,1024]{1,0:T(8,128)(2,1)}, u32[]{:S(2)}) copy-start(bf16[128,1024]{1,0:T(8,128)(2,1)} %param.9) | copy-start | bytes 786436
  1.7 24.6 %copy-start.5 = (bf16[256,1152]{1,0:T(8,128)(2,1)S(1)}, bf16[256,1152]{1,0:T(8,128)(2,1)}, u32[]{:S(2)}) copy-start(bf16[256,1152]{1,0:T(8,128)(2,1)} %param.10) | copy-start | bytes 1769476
  2.9 27.9 %collective-permute-start.2 = (bf16[128,1152]{0,1:T(8,128)(2,1)}, bf16[128,1152]{0,1:T(8,128)(2,1)}, u32[]{:S(2)}, u32[]{:S(2)}) collective-permute-start(bf16[128,1152]{0,1:T(8,128)(2,1)} %get-tuple-element.14), channel_id=1, source_target_pairs={{4,0},{6,2},{8,4},{10,6},{12,8},{14,10},{16,12},{18,14},{20,16},{2... | collective-permute-start | bytes 884744 | tf_op jit(solution)/shard_map/ppermute | solution.py:20
  23.4 9.0 %collective-permute-start = (bf16[128,1152]{0,1:T(8,128)(2,1)}, bf16[128,1152]{0,1:T(8,128)(2,1)}, u32[]{:S(2)}, u32[]{:S(2)}) collective-permute-start(bf16[128,1152]{0,1:T(8,128)(2,1)} %get-tuple-element.14), channel_id=1, source_target_pairs={{2,0},{4,2},{6,4},{8,6},{10,8},{12,10},{14,12},{16,14},{18,16},{20... | collective-permute-start | bytes 884744 | tf_op jit(solution)/shard_map/ppermute | solution.py:20
  34.9 19.1 %copy-start.4 = (bf16[128,1024]{1,0:T(8,128)(2,1)S(1)}, bf16[128,1024]{1,0:T(8,128)(2,1)}, u32[]{:S(2)}) copy-start(bf16[128,1024]{1,0:T(8,128)(2,1)} %param.9) | copy-start | bytes 786436
  36.0 7.3 %collective-permute-start.4 = (f32[136,128]{0,1:T(8,128)S(1)}, f32[136,128]{0,1:T(8,128)S(1)}, u32[]{:S(2)}, u32[]{:S(2)}) collective-permute-start(f32[136,128]{0,1:T(8,128)S(1)} %pad_maximum_fusion.5), channel_id=1, source_target_pairs={{0,1},{1,0},{2,3},{3,2},{4,5},{5,4},{6,7},{7,6},{8,9},{9,8},{10,11... | collective-permute-start | bytes 208904 | tf_op jit(solution)/shard_map/ppermute | solution.py:268
  38.4 15.4 %collective-permute-start.3 = (f32[136,128]{0,1:T(8,128)S(1)}, f32[136,128]{0,1:T(8,128)S(1)}, u32[]{:S(2)}, u32[]{:S(2)}) collective-permute-start(f32[136,128]{0,1:T(8,128)S(1)} %pad_maximum_fusion.4), channel_id=1, source_target_pairs={{764,0},{766,2},{0,4},{2,6},{4,8},{6,10},{8,12},{10,14},{12,16},{1... | collective-permute-start | bytes 208904 | tf_op jit(solution)/shard_map/ppermute | solution.py:20
  40.4 13.4 %collective-permute-start.1 = (f32[136,128]{0,1:T(8,128)S(1)}, f32[136,128]{0,1:T(8,128)S(1)}, u32[]{:S(2)}, u32[]{:S(2)}) collective-permute-start(f32[136,128]{0,1:T(8,128)S(1)} %pad_maximum_fusion.3), channel_id=1, source_target_pairs={{766,0},{0,2},{2,4},{4,6},{6,8},{8,10},{10,12},{12,14},{14,16},{16... | collective-permute-start | bytes 208904 | tf_op jit(solution)/shard_map/ppermute | solution.py:20
  55.4 1.0 %copy-start.1 = (f32[1,1024,128]{2,1,0:T(8,128)S(1)}, f32[1,1024,128]{2,1,0:T(8,128)}, u32[]{:S(2)}) copy-start(f32[1,1024,128]{2,1,0:T(8,128)} %param.15) | copy-start | bytes 1572868
  55.4 1.0 %copy-start.2 = (f32[1,128,128]{2,1,0:T(8,128)S(1)}, f32[1,128,128]{2,1,0:T(8,128)}, u32[]{:S(2)}) copy-start(f32[1,128,128]{2,1,0:T(8,128)} %param.14) | copy-start | bytes 196612

commit v2 on v0

v2 whole, which is shorter than its diff:
```python
import jax
import jax.numpy as jnp
from jax import lax
from jax.experimental import pallas as pl
from jax.experimental.pallas import tpu as pltpu
from jax.sharding import PartitionSpec as P

NX, NY, NZ, NDP = 2, 8, 12, 384
D, BLK, EDGE = 1152, 1024, 128
ROWS, TXT = 128, 256
MESH = pl.DeviceIdType.MESH
F32 = jnp.float32
BF16 = jnp.bfloat16
YORDER = (4, 3, 5, 2, 6, 1, 7)
ZORDER = (6, 5, 7, 4, 8, 3, 9, 2, 10, 1, 11)


def rows_at(start, size):
    return pl.ds(pl.multiple_of(start, size), size)


def dot(a, b, dims=(1, 0)):
    return lax.dot_general(
        a, b, (((dims[0],), (dims[1],)), ((), ())), preferred_element_type=F32
    )


def kernel(
    img_resid, img_hidden, txt_resid, txt_hidden, edge_weight, left_hbm, right_hbm, acc_hbm,
    out_ref,
    ir, ih, tr, th, ew, left, right, acc,
    emb, idir, ilen, temb, tdir, tlen, vis, back, back_in, tout, tin, iht, tht, lhi, llo,
    p, cbuf, acc1, xsend, xbuf, acc2, ysend, ybuf, zbuf, gbuf, cond,
    load_sem, vs_sem, vr_sem, bs_sem, br_sem, ts_sem, tr_sem,
    cs_sem, cr_sem, xs_sem, xr_sem, ys_sem, yr_sem, zs_sem, zr_sem,
    gs_sem, gr_sem, hs_sem, hr_sem, ks_sem, kr_sem,
):
    dp = lax.axis_index("dp")
    xl = lax.axis_index("opt")
    core = lax.rem(dp, 2)
    y = lax.rem(lax.div(dp, 2), NY)
    z = lax.rem(lax.div(dp, 2 * NY), NZ)
    xh = lax.div(dp, 2 * NY * NZ)
    oc = 1 - core

    def at(xh=xh, z=z, y=y, core=core, xl=xl):
        return (((xh * NZ + z) * NY + y) * 2 + core, xl)

    loads = []
    for n, (src, dst) in enumerate([
        (img_hidden, ih), (edge_weight.at[0], ew.at[0]), (img_resid, ir),
        (txt_hidden, th), (edge_weight.at[1], ew.at[1]), (txt_resid, tr),
        (left_hbm, left), (right_hbm, right), (acc_hbm, acc),
    ]):
        c = pltpu.make_async_copy(src, dst, load_sem.at[n])
        c.start()
        loads.append(c)

    x = xh * 2 + xl
    xpeer = []
    for k in range(1, 4):
        px = lax.rem(x + k, 4)
        xpeer.append((px, at(xh=lax.div(px, 2), xl=lax.rem(px, 2))))
    ypeer = [(lax.rem(y + k, NY), at(y=lax.rem(y + k, NY))) for k in range(1, NY)]
    zpeer = [(lax.rem(z + k, NZ), at(z=lax.rem(z + k, NZ))) for k in range(1, NZ)]
    cpeer = at(core=oc)
    hpeer = at(xh=1 - xh)
    opeer = (dp, 1 - xl)
    before = [(lax.rem(dp + NDP - c, NDP), xl) for c in (1, 2)]
    after = [(lax.rem(dp + c, NDP), xl) for c in (1, 2)]
    side = (lax.rem(dp + NDP + 2 * core - 1, NDP), xl)

    barrier = pltpu.get_barrier_semaphore()
    peers = [before[1], after[1], side, cpeer] + [d for _, d in xpeer + ypeer + zpeer]
    for d in peers:
        pl.semaphore_signal(barrier, inc=1, device_id=d, device_id_type=MESH)

    def remote(src, dst, s, r, d):
        return pltpu.make_async_remote_copy(
            src_ref=src, dst_ref=dst, send_sem=s, recv_sem=r, device_id=d, device_id_type=MESH
        )

    sent = []

    def send(*args):
        c = remote(*args)
        c.start()
        sent.append(c)
        return c

    def embed(resid, hidden, weight, emb_out, dir_out, len_out):
        edge = dot(hidden[...], weight[...]) + resid[:, BLK:].astype(F32)
        body = resid[:, :BLK].astype(F32)
        square = jnp.sum(body * body, axis=1, keepdims=True) + jnp.sum(
            edge * edge, axis=1, keepdims=True
        )
        length = jnp.sqrt(square + 1e-06)
        inverse = 1.0 / length
        emb_out[:, :BLK] = (body * inverse).astype(BF16)
        direction = edge * inverse
        emb_out[:, BLK:] = direction.astype(BF16)
        dir_out[...] = direction
        len_out[...] = jnp.broadcast_to(inverse, len_out.shape)

    for n in range(3):
        loads[n].wait()
    embed(ir, ih, ew.at[0], emb, idir, ilen)
    pl.semaphore_wait(barrier, len(peers))

    send(emb, vis.at[1], vs_sem.at[1], vr_sem.at[1], before[1])
    pair_copy = remote(emb, vis.at[0], vs_sem.at[0], vr_sem.at[0], cpeer)

    @pl.when(core == 1)
    def _():
        pair_copy.start()

    for n in range(3, 6):
        loads[n].wait()
    embed(tr, th, ew.at[1], temb, tdir, tlen)

    def pair(view, diagonal):
        images = view[...]
        sims = dot(temb[...], images, (1, 1))
        probs = 1.0 / (1.0 + jnp.exp(2.0 - 10.0 * sims))
        if diagonal:
            text = lax.broadcasted_iota(jnp.int32, sims.shape, 0)
            image = lax.broadcasted_iota(jnp.int32, sims.shape, 1) + xl * ROWS
            probs = probs - (text == image).astype(F32)
        weights = probs.astype(BF16)
        radial = weights.astype(F32) * sims
        txt_edge = dot(weights, images[:, BLK:])
        txt_radial = jnp.sum(radial, axis=1, keepdims=True)
        img_edge = dot(weights, temb[:, BLK:], (0, 0))
        img_radial = jnp.sum(radial, axis=0, keepdims=True)
        return img_edge, img_radial, txt_edge - tdir[...] * txt_radial

    own_edge, own_radial, txt_total = pair(emb, True)
    back[2, :ROWS] = own_edge
    back[2, ROWS:] = jnp.broadcast_to(own_radial, (8, EDGE))
    tout[...] = txt_total
    iht[...] = ih[...].T
    tht[...] = th[rows_at(xl * ROWS, ROWS)].T

    for turn in range(2):
        slot = core if turn == 0 else oc
        far = remote(vis.at[slot], vis.at[slot], vs_sem.at[slot], vr_sem.at[slot], cpeer)
        far.wait_recv()
        if turn == 1:
            onward = remote(vis.at[1], vis.at[0], vs_sem.at[0], vr_sem.at[0], cpeer)

            @pl.when(core == 0)
            def _():
                onward.start()

        edge, radial, txt_edge = pair(vis.at[slot], False)
        back[slot, :ROWS] = edge
        back[slot, ROWS:] = jnp.broadcast_to(radial, (8, EDGE))
        send(
            back.at[slot], back_in.at[slot], bs_sem.at[slot], br_sem.at[slot],
            (lax.rem(dp + slot + 1, NDP), xl),
        )
        tout[...] = tout[...] + txt_edge
    sent.append(pair_copy)
    send(tout.at[rows_at((1 - xl) * ROWS, ROWS)], tin, ts_sem, tr_sem, opeer)

    loads[6].wait()

    @pl.loop(0, 8)
    def _(i):
        r = rows_at(i * 128, 128)
        value = left[r]
        high = value.astype(BF16)
        lhi[r] = high
        llo[r] = (value - high.astype(F32)).astype(BF16)

    mine = rows_at(core * 512, 512)
    theirs = rows_at(oc * 512, 512)
    for slot in range(2):
        remote(
            back.at[slot], back_in.at[slot], bs_sem.at[slot], br_sem.at[slot], cpeer
        ).wait_recv()
    total = back[2] + back_in[0] + back_in[1]
    radial = jnp.broadcast_to(total[ROWS:ROWS + 1], (ROWS, EDGE)).T
    dz = ((total[:ROWS] - idir[...] * radial) * ilen[...]).astype(BF16)
    p[0, theirs] = dot(iht[theirs], dz)
    ccopies = [send(p.at[0, theirs], cbuf.at[0], cs_sem.at[0], cr_sem.at[0], cpeer)]
    p[0, mine] = dot(iht[mine], dz)
    remote(tin, tin, ts_sem, tr_sem, opeer).wait_recv()
    own = rows_at(xl * ROWS, ROWS)
    dz = ((tout[own] + tin[...]) * tlen[own]).astype(BF16)
    p[1, theirs] = dot(tht[theirs], dz)
    ccopies.append(send(p.at[1, theirs], cbuf.at[1], cs_sem.at[1], cr_sem.at[1], cpeer))
    p[1, mine] = dot(tht[mine], dz)

    for t in range(2):
        ccopies[t].wait_recv()
        acc1[t] = p[t, mine] + cbuf[t]
    xcopies = []
    for k in (2, 1, 3):
        px, d = xpeer[k - 1]
        xsend[k - 1] = acc1[lax.rem(px, 2), rows_at(lax.div(px, 2) * 256, 256)].astype(BF16)
        xcopies.append(send(xsend.at[k - 1], xbuf.at[k - 1], xs_sem.at[k - 1], xr_sem.at[k - 1], d))
    total = acc1[xl, rows_at(xh * 256, 256)]
    for c in xcopies:
        c.wait_recv()
    for k in range(3):
        total = total + xbuf[k].astype(F32)
    acc2[...] = total
    ysend[...] = total.astype(BF16)
    ycopies = []
    for k in YORDER:
        py, d = ypeer[k - 1]
        ycopies.append(send(
            ysend.at[rows_at(py * 32, 32)], ybuf.at[k - 1], ys_sem.at[k - 1], yr_sem.at[k - 1], d
        ))
    part = acc2[rows_at(y * 32, 32)]
    for c in ycopies:
        c.wait_recv()
    for k in range(NY - 1):
        part = part + ybuf[k].astype(F32)
    zbuf[z] = part.astype(BF16)
    for k in ZORDER:
        send(zbuf.at[z], zbuf.at[z], zs_sem.at[k - 1], zr_sem.at[k - 1], zpeer[k - 1][1])
    for k in ZORDER:
        src = lax.rem(z + NZ - k, NZ)
        remote(zbuf.at[src], zbuf.at[src], zs_sem.at[k - 1], zr_sem.at[k - 1], cpeer).wait_recv()
    part = zbuf[0].astype(F32)
    for k in range(1, NZ):
        part = part + zbuf[k].astype(F32)
    base = core * 512 + xh * 256
    own = rows_at(base + y * 32, 32)
    gbuf[own] = part
    for k in YORDER:
        send(gbuf.at[own], gbuf.at[own], gs_sem.at[k - 1], gr_sem.at[k - 1], ypeer[k - 1][1])
    for k in YORDER:
        src = lax.rem(y + NY - k, NY)
        r = rows_at(base + src * 32, 32)
        remote(gbuf.at[r], gbuf.at[r], gs_sem.at[k - 1], gr_sem.at[k - 1], cpeer).wait_recv()
    own = rows_at(base, 256)
    other = rows_at(core * 512 + (1 - xh) * 256, 256)
    send(gbuf.at[own], gbuf.at[own], hs_sem, hr_sem, hpeer)
    send(gbuf.at[own], gbuf.at[own], ks_sem.at[0], kr_sem.at[0], cpeer)

    def quarter(r, first):
        g = gbuf[r]
        high = g.astype(BF16)
        low = (g - high.astype(F32)).astype(BF16)
        both = jnp.concatenate([high, low], axis=1)

        @pl.loop(0, 4)
        def _(i):
            o = rows_at(i * 256, 256)
            lh = lhi[o, r]
            v = dot(lh, both)
            v = v[:, :EDGE] + v[:, EDGE:] + dot(llo[o, r], high)
            cond[o] = v if first else cond[o] + v

    quarter(own, True)
    remote(gbuf.at[other], gbuf.at[other], hs_sem, hr_sem, hpeer).wait_recv()
    send(gbuf.at[other], gbuf.at[other], ks_sem.at[1], kr_sem.at[1], cpeer)
    quarter(other, False)
    for q, h in ((0, xh), (1, 1 - xh)):
        r = rows_at(oc * 512 + h * 256, 256)
        remote(gbuf.at[r], gbuf.at[r], ks_sem.at[q], kr_sem.at[q], cpeer).wait_recv()
        quarter(r, False)
    loads[7].wait()
    loads[8].wait()
    r = right[...]
    rhi = r.astype(BF16)
    rlo = (r - rhi.astype(F32)).astype(BF16)
    rboth = jnp.concatenate([rhi, rlo], axis=1)

    def body(i, sums):
        o = rows_at(i * 256, 256)
        v = cond[o]
        high = v.astype(BF16)
        low = (v - high.astype(F32)).astype(BF16)
        w = dot(high, rboth)
        w = w[:, :EDGE] + w[:, EDGE:] + dot(low, rhi)
        cond[o] = w
        g = gbuf[o]
        return sums[0] + jnp.sum(g * g / (acc[o] + g * g)), sums[1] + jnp.sum(w * w)

    gsum, csum = lax.fori_loop(0, 4, body, (jnp.float32(0.0), jnp.float32(0.0)))
    factor = jnp.sqrt(gsum) / jnp.sqrt(csum + 1e-06)
    out_ref[...] = cond[...] * factor
    for c in sent:
        c.wait_send()


def on_device(*args):
    dma = pltpu.SemaphoreType.DMA
    hbm = pl.BlockSpec(memory_space=pl.ANY)

    def f32(*shape):
        return pltpu.VMEM(shape, F32)

    def bf16(*shape):
        return pltpu.VMEM(shape, BF16)

    args = args[:5] + tuple(a.reshape(a.shape[1:]) for a in args[5:])
    out = pl.pallas_call(
        kernel,
        out_shape=jax.ShapeDtypeStruct((BLK, EDGE), F32),
        in_specs=[hbm] * 8,
        out_specs=pl.BlockSpec(memory_space=pltpu.VMEM),
        scratch_shapes=[
            bf16(ROWS, D), bf16(ROWS, BLK), bf16(TXT, D), bf16(TXT, BLK), bf16(2, BLK, EDGE),
            f32(BLK, BLK), f32(EDGE, EDGE), f32(BLK, EDGE),
            bf16(ROWS, D), f32(ROWS, EDGE), f32(ROWS, EDGE),
            bf16(TXT, D), f32(TXT, EDGE), f32(TXT, EDGE),
            bf16(2, ROWS, D), f32(3, ROWS + 8, EDGE), f32(2, ROWS + 8, EDGE),
            f32(TXT, EDGE), f32(ROWS, EDGE), bf16(BLK, ROWS), bf16(BLK, ROWS),
            bf16(BLK, BLK), bf16(BLK, BLK),
            f32(2, BLK, EDGE), f32(2, 512, EDGE), f32(2, 512, EDGE),
            bf16(3, 256, EDGE), bf16(3, 256, EDGE), f32(256, EDGE),
            bf16(256, EDGE), bf16(NY - 1, 32, EDGE), bf16(NZ, 32, EDGE),
            f32(BLK, EDGE), f32(BLK, EDGE),
            dma((9,)), dma((2,)), dma((2,)), dma((2,)), dma((2,)), dma, dma,
            dma((2,)), dma((2,)), dma((3,)), dma((3,)), dma((NY - 1,)), dma((NY - 1,)),
            dma((NZ - 1,)), dma((NZ - 1,)), dma((NY - 1,)), dma((NY - 1,)),
            dma, dma, dma((2,)), dma((2,)),
        ],
        compiler_params=pltpu.CompilerParams(
            collective_id=0, has_side_effects=True, vmem_limit_bytes=48 << 20
        ),
    )(*args)
    return out[None]


def solution(mesh):
    placed = (
        P(("dp", "opt"), None),
        P(("dp", "opt"), None),
        P("dp", None),
        P("dp", None),
        P(),
        P("opt", None, None),
        P("opt", None, None),
        P("opt", None, None),
    )
    return jax.shard_map(
        on_device, mesh=mesh, in_specs=placed, out_specs=P("opt", None, None), check_vma=False
    )
```

time: 645 us -> 73.9 us (0.11)
  waiting for transfers between devices: 554 us -> 0 us
  Pallas kernels: 0 us -> 65.7 us
  starting transfers between devices: 36.5 us -> 0 us
  matrix products: 23.5 us -> 0 us
  between operations: 15.1 us -> 0.02 us
  other arithmetic: 9.59 us -> 0 us
    psum x1 -> x0, waiting for transfers between devices: 471 us -> none  [on_device(): summed = lax.psum(local_terms, ('dp', 'opt'))]
    pallas_call x0 -> x1, Pallas kernels: none -> 65.7 us  [on_device(): pl.pallas_call(kernel, out_shape=jax.ShapeDtypeStruct((BLK, EDGE), F32),...]
    ppermute x5 -> x0, waiting for transfers between devices: 59.9 us -> none  [shifted(): return lax.ppermute(block, axis, route)]
    ppermute x5 -> x0, starting transfers between devices: 36.5 us -> none  [shifted(): return lax.ppermute(block, axis, route)]
    dot_general x15 -> x0, matrix products: 23.5 us -> none  [the longest x1 6.59 us: precondition(): jnp.dot(left_mat, block_grad, precision=highest)]
    reduce_scatter x1 -> x0, waiting for transfers between devices: 23.5 us -> none  [on_device(): lax.psum_scatter(txt_part, 'opt', scatter_dimension=0, tiled=True)]
  transfers between devices with their start and end apart: 7 -> 0, of which waited for: 5 -> 0; matrix products, arithmetic and copies ran while one was open for 1% -> 0% of each run, Pallas kernels for 0% -> 0%
where the time goes in v2:
time: 73.9 us; the launch traced here: 73.5 us
  Pallas kernels  65.7 us (89%)
  local copies, waits for them, and re-layouts  7.73 us (10%)
    pallas_call x1, Pallas kernels, on_device(): pl.pallas_call(kernel, out_shape=jax.ShapeDtypeStruct((BLK, EDGE), F32),...  65.7 us
    unnamed x15, local copies, waits for them, and re-layouts  7.73 us

profile of v2, /device:TPU:1, one launch (start us, length us, event | category | flops | bytes accessed | tf_op | source)
XLA Modules:
  0.0 73.5 jit_solution(15522822298046275987)
XLA Ops:
  0.0 0.0 copy-start
  0.0 1.1 %copy-done = bf16[256,1152]{1,0:T(8,128)(2,1)S(1)} copy-done((bf16[256,1152]{1,0:T(8,128)(2,1)S(1)}, bf16[256,1152]{1,0:T(8,128)(2,1)}, u32[]{:S(2)}) %copy-start) | copy-done | bytes 589848
  1.1 0.0 copy-start.1
  1.1 1.0 %copy-done.1 = bf16[256,1024]{1,0:T(8,128)(2,1)S(1)} copy-done((bf16[256,1024]{1,0:T(8,128)(2,1)S(1)}, bf16[256,1024]{1,0:T(8,128)(2,1)}, u32[]{:S(2)}) %copy-start.1) | copy-done | bytes 524312
  2.1 0.0 copy-start.2
  2.1 1.0 %copy-done.2 = bf16[2,1024,128]{2,1,0:T(8,128)(2,1)S(1)} copy-done((bf16[2,1024,128]{2,1,0:T(8,128)(2,1)S(1)}, bf16[2,1024,128]{2,1,0:T(8,128)(2,1)}, u32[]{:S(2)}) %copy-start.2) | copy-done | bytes 524312
  3.1 0.0 copy-start.3
  3.2 1.0 %copy-done.3 = f32[1,1024,128]{2,1,0:T(8,128)S(1)} copy-done((f32[1,1024,128]{2,1,0:T(8,128)S(1)}, f32[1,1024,128]{2,1,0:T(8,128)}, u32[]{:S(2)}) %copy-start.3) | copy-done | bytes 524312
  4.2 0.0 copy-start.4
  4.2 1.0 %copy-done.4 = bf16[128,1152]{1,0:T(8,128)(2,1)S(1)} copy-done((bf16[128,1152]{1,0:T(8,128)(2,1)S(1)}, bf16[128,1152]{1,0:T(8,128)(2,1)}, u32[]{:S(2)}) %copy-start.4) | copy-done | bytes 294936
  5.2 0.0 copy-start.5
  5.2 0.9 %copy-done.5 = bf16[128,1024]{1,0:T(8,128)(2,1)S(1)} copy-done((bf16[128,1024]{1,0:T(8,128)(2,1)S(1)}, bf16[128,1024]{1,0:T(8,128)(2,1)}, u32[]{:S(2)}) %copy-start.5) | copy-done | bytes 262168
  6.1 0.0 copy-start.6
  6.1 0.8 %copy-done.6 = f32[1,128,128]{2,1,0:T(8,128)S(1)} copy-done((f32[1,128,128]{2,1,0:T(8,128)S(1)}, f32[1,128,128]{2,1,0:T(8,128)}, u32[]{:S(2)}) %copy-start.6) | copy-done | bytes 65560
  6.9 65.7 %shard_map.82 = f32[1024,128]{1,0:T(8,128)S(1)} custom-call(bf16[128,1152]{1,0:T(8,128)(2,1)S(1)} %copy-done.4, bf16[128,1024]{1,0:T(8,128)(2,1)S(1)} %copy-done.5, bf16[256,1152]{1,0:T(8,128)(2,1)S(1)} %copy-done, bf16[256,1024]{1,0:T(8,128)(2,1)S(1)} %copy-done.1, bf16[2,1024,128]{2,1,0:T(8,128)(2,1)S(1)} %copy-done.2, f32[1024,1024]{1,0:T(8,128)} %bitcast.7, ...), custom_call_target="tpu_custom_call" | custom-call | tf_op jit(solution)/shard_map/pallas_call | solution.py:302
  72.7 0.8 %copy.10 = f32[1,1024,128]{2,1,0:T(8,128)} copy(f32[1,1024,128]{2,1,0:T(8,128)S(1)} %bitcast.4) | data formatting | bytes 1048576
Async XLA Ops:
  0.0 1.1 %copy-start = (bf16[256,1152]{1,0:T(8,128)(2,1)S(1)}, bf16[256,1152]{1,0:T(8,128)(2,1)}, u32[]{:S(2)}) copy-start(bf16[256,1152]{1,0:T(8,128)(2,1)} %txt_resid.1) | copy-start | bytes 1769476
  1.1 1.0 %copy-start.1 = (bf16[256,1024]{1,0:T(8,128)(2,1)S(1)}, bf16[256,1024]{1,0:T(8,128)(2,1)}, u32[]{:S(2)}) copy-start(bf16[256,1024]{1,0:T(8,128)(2,1)} %txt_hidden.1) | copy-start | bytes 1572868
  2.1 1.0 %copy-start.2 = (bf16[2,1024,128]{2,1,0:T(8,128)(2,1)S(1)}, bf16[2,1024,128]{2,1,0:T(8,128)(2,1)}, u32[]{:S(2)}) copy-start(bf16[2,1024,128]{2,1,0:T(8,128)(2,1)} %edge_weight.1) | copy-start | bytes 1572868
  3.1 1.0 %copy-start.3 = (f32[1,1024,128]{2,1,0:T(8,128)S(1)}, f32[1,1024,128]{2,1,0:T(8,128)}, u32[]{:S(2)}) copy-start(f32[1,1024,128]{2,1,0:T(8,128)} %param.15) | copy-start | bytes 1572868
  4.2 1.0 %copy-start.4 = (bf16[128,1152]{1,0:T(8,128)(2,1)S(1)}, bf16[128,1152]{1,0:T(8,128)(2,1)}, u32[]{:S(2)}) copy-start(bf16[128,1152]{1,0:T(8,128)(2,1)} %img_resid.1) | copy-start | bytes 884740
  5.2 0.9 %copy-start.5 = (bf16[128,1024]{1,0:T(8,128)(2,1)S(1)}, bf16[128,1024]{1,0:T(8,128)(2,1)}, u32[]{:S(2)}) copy-start(bf16[128,1024]{1,0:T(8,128)(2,1)} %img_hidden.1) | copy-start | bytes 786436
  6.1 0.8 %copy-start.6 = (f32[1,128,128]{2,1,0:T(8,128)S(1)}, f32[1,128,128]{2,1,0:T(8,128)}, u32[]{:S(2)}) copy-start(f32[1,128,128]{2,1,0:T(8,128)} %param.14) | copy-start | bytes 196612

commit v3 on v2

--- a/solution.py
+++ b/solution.py
@@ -27,10 +27,10 @@
 
 def kernel(
     img_resid, img_hidden, txt_resid, txt_hidden, edge_weight, left_hbm, right_hbm, acc_hbm,
-    out_ref,
+    out_ref, factor_ref,
     ir, ih, tr, th, ew, left, right, acc,
     emb, idir, ilen, temb, tdir, tlen, vis, back, back_in, tout, tin, iht, tht, lhi, llo,
-    p, cbuf, acc1, xsend, xbuf, acc2, ysend, ybuf, zbuf, gbuf, cond,
+    p, cbuf, acc1, xsend, xbuf, acc2, ysend, ybuf, zsend, zbuf, gbuf, cond,
     load_sem, vs_sem, vr_sem, bs_sem, br_sem, ts_sem, tr_sem,
     cs_sem, cr_sem, xs_sem, xr_sem, ys_sem, yr_sem, zs_sem, zr_sem,
     gs_sem, gr_sem, hs_sem, hr_sem, ks_sem, kr_sem,
@@ -66,12 +66,18 @@
     cpeer = at(core=oc)
     hpeer = at(xh=1 - xh)
     opeer = (dp, 1 - xl)
-    before = [(lax.rem(dp + NDP - c, NDP), xl) for c in (1, 2)]
-    after = [(lax.rem(dp + c, NDP), xl) for c in (1, 2)]
-    side = (lax.rem(dp + NDP + 2 * core - 1, NDP), xl)
+
+    def along(c):
+        there = lax.rem(dp + NDP + c, NDP)
+        return there, lax.rem(xl + xh + lax.div(there, 2 * NY * NZ), 2)
+
+    after = [along(1), along(2)]
+    side = along(2 * core - 1)
+    zn = z + 1 - 2 * lax.rem(z, 2)
+    npeer = [hpeer, at(z=zn), at(xh=1 - xh, z=zn)]
 
     barrier = pltpu.get_barrier_semaphore()
-    peers = [before[1], after[1], side, cpeer] + [d for _, d in xpeer + ypeer + zpeer]
+    peers = [along(-2), after[1], side, cpeer, npeer[2]] + [d for _, d in xpeer + ypeer + zpeer]
     for d in peers:
         pl.semaphore_signal(barrier, inc=1, device_id=d, device_id_type=MESH)
 
@@ -107,16 +113,25 @@
     embed(ir, ih, ew.at[0], emb, idir, ilen)
     pl.semaphore_wait(barrier, len(peers))
 
-    send(emb, vis.at[1], vs_sem.at[1], vr_sem.at[1], before[1])
-    pair_copy = remote(emb, vis.at[0], vs_sem.at[0], vr_sem.at[0], cpeer)
+    far_copy = remote(emb, vis.at[1], vs_sem.at[1], vr_sem.at[1], along(-2))
+    near_copy = remote(emb, vis.at[0], vs_sem.at[0], vr_sem.at[0], cpeer)
+    onward = remote(vis.at[1], vis.at[0], vs_sem.at[0], vr_sem.at[0], cpeer)
+
+    @pl.when(core == 0)
+    def _():
+        far_copy.start()
 
     @pl.when(core == 1)
     def _():
-        pair_copy.start()
+        near_copy.start()
 
     for n in range(3, 6):
         loads[n].wait()
     embed(tr, th, ew.at[1], temb, tdir, tlen)
+
+    @pl.when(core == 1)
+    def _():
+        far_copy.start()
 
     def pair(view, diagonal):
         images = view[...]
@@ -138,40 +153,30 @@
     back[2, :ROWS] = own_edge
     back[2, ROWS:] = jnp.broadcast_to(own_radial, (8, EDGE))
     tout[...] = txt_total
-    iht[...] = ih[...].T
-    tht[...] = th[rows_at(xl * ROWS, ROWS)].T
-
-    for turn in range(2):
-        slot = core if turn == 0 else oc
-        far = remote(vis.at[slot], vis.at[slot], vs_sem.at[slot], vr_sem.at[slot], cpeer)
-        far.wait_recv()
-        if turn == 1:
-            onward = remote(vis.at[1], vis.at[0], vs_sem.at[0], vr_sem.at[0], cpeer)
-
-            @pl.when(core == 0)
+
+    @pl.when(core == 0)
+    def _():
+        far_copy.wait_recv()
+        onward.start()
+
+    for slot in range(2):
+        if slot == 0:
+            near_copy.wait_recv()
+        else:
+            @pl.when(core == 1)
             def _():
-                onward.start()
+                far_copy.wait_recv()
 
         edge, radial, txt_edge = pair(vis.at[slot], False)
         back[slot, :ROWS] = edge
         back[slot, ROWS:] = jnp.broadcast_to(radial, (8, EDGE))
-        send(
-            back.at[slot], back_in.at[slot], bs_sem.at[slot], br_sem.at[slot],
-            (lax.rem(dp + slot + 1, NDP), xl),
-        )
+        send(back.at[slot], back_in.at[slot], bs_sem.at[slot], br_sem.at[slot], after[slot])
         tout[...] = tout[...] + txt_edge
-    sent.append(pair_copy)
+    sent.append(far_copy)
+    sent.append(near_copy)
     send(tout.at[rows_at((1 - xl) * ROWS, ROWS)], tin, ts_sem, tr_sem, opeer)
-
-    loads[6].wait()
-
-    @pl.loop(0, 8)
-    def _(i):
-        r = rows_at(i * 128, 128)
-        value = left[r]
-        high = value.astype(BF16)
-        lhi[r] = high
-        llo[r] = (value - high.astype(F32)).astype(BF16)
+    iht[...] = ih[...].T
+    tht[...] = th[rows_at(xl * ROWS, ROWS)].T
 
     mine = rows_at(core * 512, 512)
     theirs = rows_at(oc * 512, 512)
@@ -194,16 +199,34 @@
 
     for t in range(2):
         ccopies[t].wait_recv()
-        acc1[t] = p[t, mine] + cbuf[t]
-    xcopies = []
-    for k in (2, 1, 3):
-        px, d = xpeer[k - 1]
-        xsend[k - 1] = acc1[lax.rem(px, 2), rows_at(lax.div(px, 2) * 256, 256)].astype(BF16)
-        xcopies.append(send(xsend.at[k - 1], xbuf.at[k - 1], xs_sem.at[k - 1], xr_sem.at[k - 1], d))
-    total = acc1[xl, rows_at(xh * 256, 256)]
-    for c in xcopies:
+        acc1[t] = (p[t, mine] + cbuf[t]).reshape(NY, 2, 32, EDGE)
+        for h in (1, 0):
+            k = lax.rem(2 * h + t + 4 - x, 4)
+            slot = lax.max(k - 1, 0)
+
+            @pl.when(k > 0)
+            def _():
+                xsend[slot] = acc1[t, :, h].astype(BF16)
+                remote(
+                    xsend.at[slot], xbuf.at[slot], xs_sem.at[slot], xr_sem.at[slot],
+                    at(xh=h, xl=t),
+                ).start()
+
+    loads[6].wait()
+
+    @pl.loop(0, 8)
+    def _(i):
+        r = rows_at(i * 128, 128)
+        value = left[r]
+        high = value.astype(BF16)
+        lhi[r] = high
+        llo[r] = (value - high.astype(F32)).astype(BF16)
+
+    total = acc1[xl, :, xh]
+    for k in range(3):
+        c = remote(xsend.at[k], xbuf.at[k], xs_sem.at[k], xr_sem.at[k], cpeer)
         c.wait_recv()
-    for k in range(3):
+        sent.append(c)
         total = total + xbuf[k].astype(F32)
     acc2[...] = total
     ysend[...] = total.astype(BF16)
@@ -211,60 +234,58 @@
     for k in YORDER:
         py, d = ypeer[k - 1]
         ycopies.append(send(
-            ysend.at[rows_at(py * 32, 32)], ybuf.at[k - 1], ys_sem.at[k - 1], yr_sem.at[k - 1], d
+            ysend.at[py], ybuf.at[k - 1], ys_sem.at[k - 1], yr_sem.at[k - 1], d
         ))
-    part = acc2[rows_at(y * 32, 32)]
+    part = acc2[y]
     for c in ycopies:
         c.wait_recv()
     for k in range(NY - 1):
         part = part + ybuf[k].astype(F32)
-    zbuf[z] = part.astype(BF16)
+    zsend[...] = part.astype(BF16).reshape(2, 16, EDGE)
     for k in ZORDER:
-        send(zbuf.at[z], zbuf.at[z], zs_sem.at[k - 1], zr_sem.at[k - 1], zpeer[k - 1][1])
+        pz, d = zpeer[k - 1]
+        send(zsend.at[lax.rem(pz, 2)], zbuf.at[z], zs_sem.at[k - 1], zr_sem.at[k - 1], d)
+    zh = lax.rem(z, 2)
+    zbuf[z] = zsend[zh]
     for k in ZORDER:
         src = lax.rem(z + NZ - k, NZ)
         remote(zbuf.at[src], zbuf.at[src], zs_sem.at[k - 1], zr_sem.at[k - 1], cpeer).wait_recv()
     part = zbuf[0].astype(F32)
     for k in range(1, NZ):
         part = part + zbuf[k].astype(F32)
-    base = core * 512 + xh * 256
-    own = rows_at(base + y * 32, 32)
-    gbuf[own] = part
+    at_y = core * NY + y
+    gbuf[at_y, xh, zh] = part.astype(BF16)
+    own = gbuf.at[at_y, xh, zh]
+    for k, d in enumerate(npeer):
+        send(own, own, hs_sem.at[k], hr_sem.at[k], d)
+    for k, (h, q) in enumerate(((1 - xh, zh), (xh, 1 - zh), (1 - xh, 1 - zh))):
+        came = gbuf.at[at_y, h, q]
+        remote(came, came, hs_sem.at[k], hr_sem.at[k], cpeer).wait_recv()
+    own = gbuf.at[at_y]
     for k in YORDER:
-        send(gbuf.at[own], gbuf.at[own], gs_sem.at[k - 1], gr_sem.at[k - 1], ypeer[k - 1][1])
+        send(own, own, gs_sem.at[k - 1], gr_sem.at[k - 1], ypeer[k - 1][1])
     for k in YORDER:
-        src = lax.rem(y + NY - k, NY)
-        r = rows_at(base + src * 32, 32)
-        remote(gbuf.at[r], gbuf.at[r], gs_sem.at[k - 1], gr_sem.at[k - 1], cpeer).wait_recv()
-    own = rows_at(base, 256)
-    other = rows_at(core * 512 + (1 - xh) * 256, 256)
-    send(gbuf.at[own], gbuf.at[own], hs_sem, hr_sem, hpeer)
-    send(gbuf.at[own], gbuf.at[own], ks_sem.at[0], kr_sem.at[0], cpeer)
-
-    def quarter(r, first):
-        g = gbuf[r]
-        high = g.astype(BF16)
-        low = (g - high.astype(F32)).astype(BF16)
-        both = jnp.concatenate([high, low], axis=1)
+        came = gbuf.at[core * NY + lax.rem(y + NY - k, NY)]
+        remote(came, came, gs_sem.at[k - 1], gr_sem.at[k - 1], cpeer).wait_recv()
+    own = gbuf.at[pl.ds(core * NY, NY)]
+    send(own, own, ks_sem, kr_sem, cpeer)
+
+    def half(c, first):
+        g = gbuf[pl.ds(c * NY, NY)].reshape(512, EDGE)
+        r = rows_at(c * 512, 512)
 
         @pl.loop(0, 4)
         def _(i):
             o = rows_at(i * 256, 256)
-            lh = lhi[o, r]
-            v = dot(lh, both)
-            v = v[:, :EDGE] + v[:, EDGE:] + dot(llo[o, r], high)
+            v = dot(lhi[o, r], g) + dot(llo[o, r], g)
             cond[o] = v if first else cond[o] + v
 
-    quarter(own, True)
-    remote(gbuf.at[other], gbuf.at[other], hs_sem, hr_sem, hpeer).wait_recv()
-    send(gbuf.at[other], gbuf.at[other], ks_sem.at[1], kr_sem.at[1], cpeer)
-    quarter(other, False)
-    for q, h in ((0, xh), (1, 1 - xh)):
-        r = rows_at(oc * 512 + h * 256, 256)
-        remote(gbuf.at[r], gbuf.at[r], ks_sem.at[q], kr_sem.at[q], cpeer).wait_recv()
-        quarter(r, False)
+    half(core, True)
     loads[7].wait()
     loads[8].wait()
+    other = gbuf.at[pl.ds(oc * NY, NY)]
+    remote(other, other, ks_sem, kr_sem, cpeer).wait_recv()
+    half(oc, False)
     r = right[...]
     rhi = r.astype(BF16)
     rlo = (r - rhi.astype(F32)).astype(BF16)
@@ -277,13 +298,13 @@
         low = (v - high.astype(F32)).astype(BF16)
         w = dot(high, rboth)
         w = w[:, :EDGE] + w[:, EDGE:] + dot(low, rhi)
-        cond[o] = w
-        g = gbuf[o]
+        out_ref[o] = w
+        g = gbuf[pl.ds(i * 4, 4)].reshape(256, EDGE).astype(F32)
         return sums[0] + jnp.sum(g * g / (acc[o] + g * g)), sums[1] + jnp.sum(w * w)
 
     gsum, csum = lax.fori_loop(0, 4, body, (jnp.float32(0.0), jnp.float32(0.0)))
     factor = jnp.sqrt(gsum) / jnp.sqrt(csum + 1e-06)
-    out_ref[...] = cond[...] * factor
+    factor_ref[...] = jnp.broadcast_to(factor, factor_ref.shape)
     for c in sent:
         c.wait_send()
 
@@ -299,11 +320,13 @@
         return pltpu.VMEM(shape, BF16)
 
     args = args[:5] + tuple(a.reshape(a.shape[1:]) for a in args[5:])
-    out = pl.pallas_call(
+    out, factor = pl.pallas_call(
         kernel,
-        out_shape=jax.ShapeDtypeStruct((BLK, EDGE), F32),
+        out_shape=[
+            jax.ShapeDtypeStruct((BLK, EDGE), F32), jax.ShapeDtypeStruct((8, EDGE), F32)
+        ],
         in_specs=[hbm] * 8,
-        out_specs=pl.BlockSpec(memory_space=pltpu.VMEM),
+        out_specs=[pl.BlockSpec(memory_space=pltpu.VMEM)] * 2,
         scratch_shapes=[
             bf16(ROWS, D), bf16(ROWS, BLK), bf16(TXT, D), bf16(TXT, BLK), bf16(2, BLK, EDGE),
             f32(BLK, BLK), f32(EDGE, EDGE), f32(BLK, EDGE),
@@ -312,20 +335,20 @@
             bf16(2, ROWS, D), f32(3, ROWS + 8, EDGE), f32(2, ROWS + 8, EDGE),
             f32(TXT, EDGE), f32(ROWS, EDGE), bf16(BLK, ROWS), bf16(BLK, ROWS),
             bf16(BLK, BLK), bf16(BLK, BLK),
-            f32(2, BLK, EDGE), f32(2, 512, EDGE), f32(2, 512, EDGE),
-            bf16(3, 256, EDGE), bf16(3, 256, EDGE), f32(256, EDGE),
-            bf16(256, EDGE), bf16(NY - 1, 32, EDGE), bf16(NZ, 32, EDGE),
-            f32(BLK, EDGE), f32(BLK, EDGE),
+            f32(2, BLK, EDGE), f32(2, 512, EDGE), f32(2, NY, 2, 32, EDGE),
+            bf16(3, NY, 32, EDGE), bf16(3, NY, 32, EDGE), f32(NY, 32, EDGE),
+            bf16(NY, 32, EDGE), bf16(NY - 1, 32, EDGE), bf16(2, 16, EDGE), bf16(NZ, 16, EDGE),
+            bf16(2 * NY, 2, 2, 16, EDGE), f32(BLK, EDGE),
             dma((9,)), dma((2,)), dma((2,)), dma((2,)), dma((2,)), dma, dma,
             dma((2,)), dma((2,)), dma((3,)), dma((3,)), dma((NY - 1,)), dma((NY - 1,)),
             dma((NZ - 1,)), dma((NZ - 1,)), dma((NY - 1,)), dma((NY - 1,)),
-            dma, dma, dma((2,)), dma((2,)),
+            dma((3,)), dma((3,)), dma, dma,
         ],
         compiler_params=pltpu.CompilerParams(
-            collective_id=0, has_side_effects=True, vmem_limit_bytes=48 << 20
+            collective_id=0, has_side_effects=True, vmem_limit_bytes=60 << 20
         ),
     )(*args)
-    return out[None]
+    return (out * factor[0, 0])[None]
 
 
 def solution(mesh):

time: 73.9 us -> 70.6 us (0.955)
  local copies, waits for them, and re-layouts: 7.73 us -> 1.25 us
  other arithmetic: 0 us -> 2.5 us
  Pallas kernels: 65.7 us -> 66.6 us
    unnamed x15 -> x0, local copies, waits for them, and re-layouts: 7.73 us -> none
    broadcast_in_dim x0 -> x1, other arithmetic: none -> 2.5 us  [on_device(): return (out * factor[0, 0])[None]]
    slice x0 -> x1, local copies, waits for them, and re-layouts: none -> 1.25 us  [on_device(): return (out * factor[0, 0])[None]]
    pallas_call x1, Pallas kernels: 65.7 us -> 66.6 us  [on_device(): pl.pallas_call(kernel, out_shape=[jax.ShapeDtypeStruct((BLK, EDGE), F32),...]
where the time goes in v3:
time: 70.6 us; the launch traced here: 70.4 us
  Pallas kernels  66.6 us (94%)
  other arithmetic  2.5 us (4%)
  local copies, waits for them, and re-layouts  1.25 us (2%)
    pallas_call x1, Pallas kernels, on_device(): pl.pallas_call(kernel, out_shape=[jax.ShapeDtypeStruct((BLK, EDGE), F32),...  66.6 us
    broadcast_in_dim x1, other arithmetic, on_device(): return (out * factor[0, 0])[None]  2.5 us

profile of v3, /device:TPU:1, one launch (start us, length us, event | category | flops | bytes accessed | tf_op | source)
XLA Modules:
  0.0 70.4 jit_solution(4406614707446893416)
XLA Ops:
  0.0 66.6 %shard_map.82 = (f32[1024,128]{1,0:T(8,128)}, f32[8,128]{1,0:T(8,128)}) custom-call(bf16[128,1152]{1,0:T(8,128)(2,1)} %img_resid.1, bf16[128,1024]{1,0:T(8,128)(2,1)} %img_hidden.1, bf16[256,1152]{1,0:T(8,128)(2,1)} %txt_resid.1, bf16[256,1024]{1,0:T(8,128)(2,1)} %txt_hidden.1, bf16[2,1024,128]{2,1,0:T(8,128)(2,1)} %edge_weight.1, f32[1024,1024]{1,0:T(8,128)} %bitcast.6, ...), custom_call_target="tpu_custom_call" | custom-call | tf_op jit(solution)/shard_map/pallas_call | solution.py:323
  66.6 1.3 %slice.3 = f32[1,1]{1,0:T(1,128)} slice(f32[8,128]{1,0:T(8,128)} %get-tuple-element.8), slice={[0:1], [0:1]} | slice | bytes 8 | tf_op jit(solution)/shard_map/slice | solution.py:351
  67.9 2.5 %multiply_bitcast_fusion = f32[1,1024,128]{2,1,0:T(8,128)} fusion(f32[1024,128]{1,0:T(8,128)} %get-tuple-element.7, f32[]{:T(128)} %bitcast.3), kind=kLoop, calls=%fused_computation | loop fusion | flops 131072 | bytes 1048580 | tf_op jit(solution)/shard_map/broadcast_in_dim | solution.py:351

commit v4 on v3

--- a/solution.py
+++ b/solution.py
@@ -27,13 +27,13 @@
 
 def kernel(
     img_resid, img_hidden, txt_resid, txt_hidden, edge_weight, left_hbm, right_hbm, acc_hbm,
-    out_ref, factor_ref,
+    out_ref,
     ir, ih, tr, th, ew, left, right, acc,
     emb, idir, ilen, temb, tdir, tlen, vis, back, back_in, tout, tin, iht, tht, lhi, llo,
-    p, cbuf, acc1, xsend, xbuf, acc2, ysend, ybuf, zsend, zbuf, gbuf, cond,
+    p, cbuf, acc1, xsend, xbuf, acc2, ysend, ybuf, zbuf, gbuf, cond, ready,
     load_sem, vs_sem, vr_sem, bs_sem, br_sem, ts_sem, tr_sem,
     cs_sem, cr_sem, xs_sem, xr_sem, ys_sem, yr_sem, zs_sem, zr_sem,
-    gs_sem, gr_sem, hs_sem, hr_sem, ks_sem, kr_sem,
+    gs_sem, gr_sem, ks_sem, kr_sem,
 ):
     dp = lax.axis_index("dp")
     xl = lax.axis_index("opt")
@@ -52,9 +52,9 @@
         (txt_hidden, th), (edge_weight.at[1], ew.at[1]), (txt_resid, tr),
         (left_hbm, left), (right_hbm, right), (acc_hbm, acc),
     ]):
-        c = pltpu.make_async_copy(src, dst, load_sem.at[n])
+        loads.append(pltpu.make_async_copy(src, dst, load_sem.at[n]))
+    for c in loads[:6]:
         c.start()
-        loads.append(c)
 
     x = xh * 2 + xl
     xpeer = []
@@ -64,7 +64,6 @@
     ypeer = [(lax.rem(y + k, NY), at(y=lax.rem(y + k, NY))) for k in range(1, NY)]
     zpeer = [(lax.rem(z + k, NZ), at(z=lax.rem(z + k, NZ))) for k in range(1, NZ)]
     cpeer = at(core=oc)
-    hpeer = at(xh=1 - xh)
     opeer = (dp, 1 - xl)
 
     def along(c):
@@ -73,11 +72,10 @@
 
     after = [along(1), along(2)]
     side = along(2 * core - 1)
-    zn = z + 1 - 2 * lax.rem(z, 2)
-    npeer = [hpeer, at(z=zn), at(xh=1 - xh, z=zn)]
 
     barrier = pltpu.get_barrier_semaphore()
-    peers = [along(-2), after[1], side, cpeer, npeer[2]] + [d for _, d in xpeer + ypeer + zpeer]
+    near = [ypeer[k - 1][1] for k in (1, 2, 6, 7)] + [zpeer[k - 1][1] for k in (1, 2, 3, 9, 10, 11)]
+    peers = [along(-2), after[1], side, cpeer] + [d for _, d in xpeer] + near
     for d in peers:
         pl.semaphore_signal(barrier, inc=1, device_id=d, device_id_type=MESH)
 
@@ -125,13 +123,13 @@
     def _():
         near_copy.start()
 
+    for d in near:
+        pl.semaphore_signal(ready, inc=1, device_id=d, device_id_type=MESH)
+    for c in loads[6:]:
+        c.start()
     for n in range(3, 6):
         loads[n].wait()
     embed(tr, th, ew.at[1], temb, tdir, tlen)
-
-    @pl.when(core == 1)
-    def _():
-        far_copy.start()
 
     def pair(view, diagonal):
         images = view[...]
@@ -153,6 +151,12 @@
     back[2, :ROWS] = own_edge
     back[2, ROWS:] = jnp.broadcast_to(own_radial, (8, EDGE))
     tout[...] = txt_total
+    iht[...] = ih[...].T
+    tht[...] = th[rows_at(xl * ROWS, ROWS)].T
+
+    @pl.when(core == 1)
+    def _():
+        far_copy.start()
 
     @pl.when(core == 0)
     def _():
@@ -175,8 +179,6 @@
     sent.append(far_copy)
     sent.append(near_copy)
     send(tout.at[rows_at((1 - xl) * ROWS, ROWS)], tin, ts_sem, tr_sem, opeer)
-    iht[...] = ih[...].T
-    tht[...] = th[rows_at(xl * ROWS, ROWS)].T
 
     mine = rows_at(core * 512, 512)
     theirs = rows_at(oc * 512, 512)
@@ -230,6 +232,7 @@
         total = total + xbuf[k].astype(F32)
     acc2[...] = total
     ysend[...] = total.astype(BF16)
+    pl.semaphore_wait(ready, len(near))
     ycopies = []
     for k in YORDER:
         py, d = ypeer[k - 1]
@@ -241,12 +244,14 @@
         c.wait_recv()
     for k in range(NY - 1):
         part = part + ybuf[k].astype(F32)
-    zsend[...] = part.astype(BF16).reshape(2, 16, EDGE)
+    zbuf[z] = part.astype(BF16)
     for k in ZORDER:
-        pz, d = zpeer[k - 1]
-        send(zsend.at[lax.rem(pz, 2)], zbuf.at[z], zs_sem.at[k - 1], zr_sem.at[k - 1], d)
-    zh = lax.rem(z, 2)
-    zbuf[z] = zsend[zh]
+        send(zbuf.at[z], zbuf.at[z], zs_sem.at[k - 1], zr_sem.at[k - 1], zpeer[k - 1][1])
+    loads[7].wait()
+    loads[8].wait()
+    value = right[...]
+    high = value.astype(BF16)
+    rboth = jnp.concatenate([high, (value - high.astype(F32)).astype(BF16)], axis=1)
     for k in ZORDER:
         src = lax.rem(z + NZ - k, NZ)
         remote(zbuf.at[src], zbuf.at[src], zs_sem.at[k - 1], zr_sem.at[k - 1], cpeer).wait_recv()
@@ -254,57 +259,46 @@
     for k in range(1, NZ):
         part = part + zbuf[k].astype(F32)
     at_y = core * NY + y
-    gbuf[at_y, xh, zh] = part.astype(BF16)
-    own = gbuf.at[at_y, xh, zh]
-    for k, d in enumerate(npeer):
-        send(own, own, hs_sem.at[k], hr_sem.at[k], d)
-    for k, (h, q) in enumerate(((1 - xh, zh), (xh, 1 - zh), (1 - xh, 1 - zh))):
-        came = gbuf.at[at_y, h, q]
-        remote(came, came, hs_sem.at[k], hr_sem.at[k], cpeer).wait_recv()
-    own = gbuf.at[at_y]
-    for k in YORDER:
-        send(own, own, gs_sem.at[k - 1], gr_sem.at[k - 1], ypeer[k - 1][1])
-    for k in YORDER:
-        came = gbuf.at[core * NY + lax.rem(y + NY - k, NY)]
-        remote(came, came, gs_sem.at[k - 1], gr_sem.at[k - 1], cpeer).wait_recv()
+    gbuf[at_y, xh] = part.astype(BF16)
+    own = gbuf.at[at_y, xh]
+    offsets = [(k, h) for k in (4, 3, 5, 2, 6, 1, 7, 0) for h in (1, 0)][:-1]
+    for n, (k, h) in enumerate(offsets):
+        d = at(y=lax.rem(y + k, NY), xh=lax.rem(xh + h, 2))
+        send(own, own, gs_sem.at[n], gr_sem.at[n], d)
+    for n, (k, h) in enumerate(offsets):
+        came = gbuf.at[core * NY + lax.rem(y + NY - k, NY), lax.rem(xh + h, 2)]
+        remote(came, came, gs_sem.at[n], gr_sem.at[n], cpeer).wait_recv()
     own = gbuf.at[pl.ds(core * NY, NY)]
     send(own, own, ks_sem, kr_sem, cpeer)
 
     def half(c, first):
         g = gbuf[pl.ds(c * NY, NY)].reshape(512, EDGE)
         r = rows_at(c * 512, 512)
-
-        @pl.loop(0, 4)
-        def _(i):
+        v = dot(g, rboth)
+        v = v[:, :EDGE] + v[:, EDGE:]
+        high = v.astype(BF16)
+        both = jnp.concatenate([high, (v - high.astype(F32)).astype(BF16)], axis=1)
+
+        def body(i, total):
             o = rows_at(i * 256, 256)
-            v = dot(lhi[o, r], g) + dot(llo[o, r], g)
-            cond[o] = v if first else cond[o] + v
-
-    half(core, True)
-    loads[7].wait()
-    loads[8].wait()
+            v = dot(lhi[o, r], both)
+            v = v[:, :EDGE] + v[:, EDGE:] + dot(llo[o, r], high)
+            if not first:
+                v = v + cond[o]
+            cond[o] = v
+            return total if first else total + jnp.sum(v * v)
+
+        csum = lax.fori_loop(0, 4, body, jnp.float32(0.0))
+        g = g.astype(F32)
+        square = g * g
+        return jnp.sum(square / (acc[r] + square)), csum
+
+    gsum, _ = half(core, True)
     other = gbuf.at[pl.ds(oc * NY, NY)]
     remote(other, other, ks_sem, kr_sem, cpeer).wait_recv()
-    half(oc, False)
-    r = right[...]
-    rhi = r.astype(BF16)
-    rlo = (r - rhi.astype(F32)).astype(BF16)
-    rboth = jnp.concatenate([rhi, rlo], axis=1)
-
-    def body(i, sums):
-        o = rows_at(i * 256, 256)
-        v = cond[o]
-        high = v.astype(BF16)
-        low = (v - high.astype(F32)).astype(BF16)
-        w = dot(high, rboth)
-        w = w[:, :EDGE] + w[:, EDGE:] + dot(low, rhi)
-        out_ref[o] = w
-        g = gbuf[pl.ds(i * 4, 4)].reshape(256, EDGE).astype(F32)
-        return sums[0] + jnp.sum(g * g / (acc[o] + g * g)), sums[1] + jnp.sum(w * w)
-
-    gsum, csum = lax.fori_loop(0, 4, body, (jnp.float32(0.0), jnp.float32(0.0)))
-    factor = jnp.sqrt(gsum) / jnp.sqrt(csum + 1e-06)
-    factor_ref[...] = jnp.broadcast_to(factor, factor_ref.shape)
+    more, csum = half(oc, False)
+    factor = jnp.sqrt(gsum + more) / jnp.sqrt(csum + 1e-06)
+    out_ref[...] = cond[...] * factor
     for c in sent:
         c.wait_send()
 
@@ -320,13 +314,11 @@
         return pltpu.VMEM(shape, BF16)
 
     args = args[:5] + tuple(a.reshape(a.shape[1:]) for a in args[5:])
-    out, factor = pl.pallas_call(
+    out = pl.pallas_call(
         kernel,
-        out_shape=[
-            jax.ShapeDtypeStruct((BLK, EDGE), F32), jax.ShapeDtypeStruct((8, EDGE), F32)
-        ],
+        out_shape=jax.ShapeDtypeStruct((BLK, EDGE), F32),
         in_specs=[hbm] * 8,
-        out_specs=[pl.BlockSpec(memory_space=pltpu.VMEM)] * 2,
+        out_specs=pl.BlockSpec(memory_space=pltpu.VMEM),
         scratch_shapes=[
             bf16(ROWS, D), bf16(ROWS, BLK), bf16(TXT, D), bf16(TXT, BLK), bf16(2, BLK, EDGE),
             f32(BLK, BLK), f32(EDGE, EDGE), f32(BLK, EDGE),
@@ -337,18 +329,18 @@
             bf16(BLK, BLK), bf16(BLK, BLK),
             f32(2, BLK, EDGE), f32(2, 512, EDGE), f32(2, NY, 2, 32, EDGE),
             bf16(3, NY, 32, EDGE), bf16(3, NY, 32, EDGE), f32(NY, 32, EDGE),
-            bf16(NY, 32, EDGE), bf16(NY - 1, 32, EDGE), bf16(2, 16, EDGE), bf16(NZ, 16, EDGE),
-            bf16(2 * NY, 2, 2, 16, EDGE), f32(BLK, EDGE),
+            bf16(NY, 32, EDGE), bf16(NY - 1, 32, EDGE), bf16(NZ, 32, EDGE),
+            bf16(2 * NY, 2, 32, EDGE), f32(BLK, EDGE), pltpu.SemaphoreType.REGULAR,
             dma((9,)), dma((2,)), dma((2,)), dma((2,)), dma((2,)), dma, dma,
             dma((2,)), dma((2,)), dma((3,)), dma((3,)), dma((NY - 1,)), dma((NY - 1,)),
-            dma((NZ - 1,)), dma((NZ - 1,)), dma((NY - 1,)), dma((NY - 1,)),
-            dma((3,)), dma((3,)), dma, dma,
+            dma((NZ - 1,)), dma((NZ - 1,)), dma((2 * NY - 1,)), dma((2 * NY - 1,)),
+            dma, dma,
         ],
         compiler_params=pltpu.CompilerParams(
             collective_id=0, has_side_effects=True, vmem_limit_bytes=60 << 20
         ),
     )(*args)
-    return (out * factor[0, 0])[None]
+    return out[None]
 
 
 def solution(mesh):

time: 70.6 us -> 64.5 us (0.914)
  Pallas kernels: 66.6 us -> 61.9 us
  other arithmetic: 2.5 us -> 0 us
    pallas_call x1, Pallas kernels: 66.6 us -> 61.9 us  [on_device(): pl.pallas_call(kernel, out_shape=jax.ShapeDtypeStruct((BLK, EDGE), F32),...]
    broadcast_in_dim x1 -> x0, other arithmetic: 2.5 us -> none  [on_device(): return (out * factor[0, 0])[None]]
    unnamed x0 -> x1, local copies, waits for them, and re-layouts: none -> 1.87 us
    slice x1 -> x0, local copies, waits for them, and re-layouts: 1.25 us -> none  [on_device(): return (out * factor[0, 0])[None]]
where the time goes in v4:
time: 64.5 us; the launch traced here: 63.8 us
  Pallas kernels  61.9 us (96%)
  local copies, waits for them, and re-layouts  1.87 us (3%)
    pallas_call x1, Pallas kernels, on_device(): pl.pallas_call(kernel, out_shape=jax.ShapeDtypeStruct((BLK, EDGE), F32),...  61.9 us
    unnamed x1, local copies, waits for them, and re-layouts  1.87 us

profile of v4, /device:TPU:1, one launch (start us, length us, event | category | flops | bytes accessed | tf_op | source)
XLA Modules:
  0.0 63.8 jit_solution(8380712135968665200)
XLA Ops:
  0.0 61.9 %shard_map.82 = f32[1024,128]{1,0:T(8,128)} custom-call(bf16[128,1152]{1,0:T(8,128)(2,1)} %img_resid.1, bf16[128,1024]{1,0:T(8,128)(2,1)} %img_hidden.1, bf16[256,1152]{1,0:T(8,128)(2,1)} %txt_resid.1, bf16[256,1024]{1,0:T(8,128)(2,1)} %txt_hidden.1, bf16[2,1024,128]{2,1,0:T(8,128)(2,1)} %edge_weight.1, f32[1024,1024]{1,0:T(8,128)} %bitcast.4, ...), custom_call_target="tpu_custom_call" | custom-call | tf_op jit(solution)/shard_map/pallas_call | solution.py:317
  61.9 1.9 %copy.10 = f32[1,1024,128]{2,1,0:T(8,128)} copy(f32[1,1024,128]{2,1,0:T(8,128)} %bitcast.5) | data formatting | bytes 1048576

commit v5 on v4

--- a/solution.py
+++ b/solution.py
@@ -29,9 +29,10 @@
     img_resid, img_hidden, txt_resid, txt_hidden, edge_weight, left_hbm, right_hbm, acc_hbm,
     out_ref,
     ir, ih, tr, th, ew, left, right, acc,
-    emb, idir, ilen, temb, tdir, tlen, vis, back, back_in, tout, tin, iht, tht, lhi, llo,
+    emb, idir, ilen, temb, tdir, tlen, vis, back, back_in, iedge, iradial, tout, tin,
+    iht, tht, lhi, llo,
     p, cbuf, acc1, xsend, xbuf, acc2, ysend, ybuf, zbuf, gbuf, cond, ready,
-    load_sem, vs_sem, vr_sem, bs_sem, br_sem, ts_sem, tr_sem,
+    load_sem, es_sem, er_sem, vs_sem, vr_sem, bs_sem, br_sem, ts_sem, tr_sem,
     cs_sem, cr_sem, xs_sem, xr_sem, ys_sem, yr_sem, zs_sem, zr_sem,
     gs_sem, gr_sem, ks_sem, kr_sem,
 ):
@@ -46,10 +47,13 @@
     def at(xh=xh, z=z, y=y, core=core, xl=xl):
         return (((xh * NZ + z) * NY + y) * 2 + core, xl)
 
+    half_rows = rows_at(xl * ROWS, ROWS)
+    other_rows = rows_at((1 - xl) * ROWS, ROWS)
     loads = []
     for n, (src, dst) in enumerate([
+        (txt_hidden.at[half_rows], th), (edge_weight.at[1], ew.at[1]),
+        (txt_resid.at[half_rows], tr),
         (img_hidden, ih), (edge_weight.at[0], ew.at[0]), (img_resid, ir),
-        (txt_hidden, th), (edge_weight.at[1], ew.at[1]), (txt_resid, tr),
         (left_hbm, left), (right_hbm, right), (acc_hbm, acc),
     ]):
         loads.append(pltpu.make_async_copy(src, dst, load_sem.at[n]))
@@ -70,12 +74,12 @@
         there = lax.rem(dp + NDP + c, NDP)
         return there, lax.rem(xl + xh + lax.div(there, 2 * NY * NZ), 2)
 
-    after = [along(1), along(2)]
+    before = [along(-1), along(-2)]
     side = along(2 * core - 1)
 
     barrier = pltpu.get_barrier_semaphore()
     near = [ypeer[k - 1][1] for k in (1, 2, 6, 7)] + [zpeer[k - 1][1] for k in (1, 2, 3, 9, 10, 11)]
-    peers = [along(-2), after[1], side, cpeer] + [d for _, d in xpeer] + near
+    peers = [along(2), before[1], side, cpeer] + [d for _, d in xpeer] + near
     for d in peers:
         pl.semaphore_signal(barrier, inc=1, device_id=d, device_id_type=MESH)
 
@@ -108,18 +112,18 @@
 
     for n in range(3):
         loads[n].wait()
-    embed(ir, ih, ew.at[0], emb, idir, ilen)
+    embed(tr, th, ew.at[1], temb, tdir, tlen)
     pl.semaphore_wait(barrier, len(peers))
 
-    far_copy = remote(emb, vis.at[1], vs_sem.at[1], vr_sem.at[1], along(-2))
-    near_copy = remote(emb, vis.at[0], vs_sem.at[0], vr_sem.at[0], cpeer)
+    far_copy = remote(temb, vis.at[1], vs_sem.at[1], vr_sem.at[1], along(2))
+    near_copy = remote(temb, vis.at[0], vs_sem.at[0], vr_sem.at[0], cpeer)
     onward = remote(vis.at[1], vis.at[0], vs_sem.at[0], vr_sem.at[0], cpeer)
 
-    @pl.when(core == 0)
+    @pl.when(core == 1)
     def _():
         far_copy.start()
 
-    @pl.when(core == 1)
+    @pl.when(core == 0)
     def _():
         near_copy.start()
 
@@ -129,72 +133,85 @@
         c.start()
     for n in range(3, 6):
         loads[n].wait()
-    embed(tr, th, ew.at[1], temb, tdir, tlen)
+    embed(ir, ih, ew.at[0], emb.at[half_rows], idir, ilen)
+    send(emb.at[half_rows], emb.at[half_rows], es_sem, er_sem, opeer)
+
+    @pl.when(core == 0)
+    def _():
+        far_copy.start()
+
+    iht[...] = ih[...].T
+    tht[...] = th[...].T
 
     def pair(view, diagonal):
-        images = view[...]
-        sims = dot(temb[...], images, (1, 1))
+        texts = view[...]
+        sims = dot(emb[...], texts, (1, 1))
         probs = 1.0 / (1.0 + jnp.exp(2.0 - 10.0 * sims))
         if diagonal:
-            text = lax.broadcasted_iota(jnp.int32, sims.shape, 0)
-            image = lax.broadcasted_iota(jnp.int32, sims.shape, 1) + xl * ROWS
+            image = lax.broadcasted_iota(jnp.int32, sims.shape, 0)
+            text = lax.broadcasted_iota(jnp.int32, sims.shape, 1) + xl * ROWS
             probs = probs - (text == image).astype(F32)
         weights = probs.astype(BF16)
         radial = weights.astype(F32) * sims
-        txt_edge = dot(weights, images[:, BLK:])
-        txt_radial = jnp.sum(radial, axis=1, keepdims=True)
-        img_edge = dot(weights, temb[:, BLK:], (0, 0))
-        img_radial = jnp.sum(radial, axis=0, keepdims=True)
-        return img_edge, img_radial, txt_edge - tdir[...] * txt_radial
-
-    own_edge, own_radial, txt_total = pair(emb, True)
-    back[2, :ROWS] = own_edge
-    back[2, ROWS:] = jnp.broadcast_to(own_radial, (8, EDGE))
-    tout[...] = txt_total
-    iht[...] = ih[...].T
-    tht[...] = th[rows_at(xl * ROWS, ROWS)].T
+        img_edge = dot(weights, texts[:, BLK:])
+        img_radial = jnp.sum(radial, axis=1, keepdims=True)
+        txt_edge = dot(weights, emb[:, BLK:], (0, 0))
+        txt_radial = jnp.sum(radial, axis=0, keepdims=True)
+        return txt_edge, txt_radial, img_edge, jnp.broadcast_to(img_radial, (TXT, EDGE))
 
     @pl.when(core == 1)
-    def _():
-        far_copy.start()
-
-    @pl.when(core == 0)
     def _():
         far_copy.wait_recv()
         onward.start()
+
+    remote(emb.at[other_rows], emb.at[other_rows], es_sem, er_sem, opeer).wait_recv()
+    own_edge, own_radial, img_edge, img_radial = pair(temb, True)
+    back[2, :ROWS] = own_edge
+    back[2, ROWS:] = jnp.broadcast_to(own_radial, (8, EDGE))
+    iedge[...] = img_edge
+    iradial[...] = img_radial
 
     for slot in range(2):
         if slot == 0:
             near_copy.wait_recv()
         else:
-            @pl.when(core == 1)
+            @pl.when(core == 0)
             def _():
                 far_copy.wait_recv()
 
-        edge, radial, txt_edge = pair(vis.at[slot], False)
+        edge, radial, img_edge, img_radial = pair(vis.at[slot], False)
         back[slot, :ROWS] = edge
         back[slot, ROWS:] = jnp.broadcast_to(radial, (8, EDGE))
-        send(back.at[slot], back_in.at[slot], bs_sem.at[slot], br_sem.at[slot], after[slot])
-        tout[...] = tout[...] + txt_edge
+        send(back.at[slot], back_in.at[slot], bs_sem.at[slot], br_sem.at[slot], before[slot])
+        iedge[...] = iedge[...] + img_edge
+        iradial[...] = iradial[...] + img_radial
     sent.append(far_copy)
     sent.append(near_copy)
-    send(tout.at[rows_at((1 - xl) * ROWS, ROWS)], tin, ts_sem, tr_sem, opeer)
+    tout[:ROWS] = iedge[other_rows]
+    tout[ROWS:] = iradial[other_rows].T[:8]
+    send(tout, tin, ts_sem, tr_sem, opeer)
 
     mine = rows_at(core * 512, 512)
     theirs = rows_at(oc * 512, 512)
+
+    def edge_dz(edge, radial, direction, inverse):
+        return ((edge - direction[...] * radial) * inverse[...]).astype(BF16)
+
+    def across(row):
+        return jnp.broadcast_to(row, (ROWS, EDGE)).T
+
+    remote(tin, tin, ts_sem, tr_sem, opeer).wait_recv()
+    radial = iradial[half_rows] + across(tin[ROWS:ROWS + 1])
+    dz = edge_dz(iedge[half_rows] + tin[:ROWS], radial, idir, ilen)
+    p[0, theirs] = dot(iht[theirs], dz)
+    ccopies = [send(p.at[0, theirs], cbuf.at[0], cs_sem.at[0], cr_sem.at[0], cpeer)]
+    p[0, mine] = dot(iht[mine], dz)
     for slot in range(2):
         remote(
             back.at[slot], back_in.at[slot], bs_sem.at[slot], br_sem.at[slot], cpeer
         ).wait_recv()
     total = back[2] + back_in[0] + back_in[1]
-    radial = jnp.broadcast_to(total[ROWS:ROWS + 1], (ROWS, EDGE)).T
-    dz = ((total[:ROWS] - idir[...] * radial) * ilen[...]).astype(BF16)
-    p[0, theirs] = dot(iht[theirs], dz)
-    ccopies = [send(p.at[0, theirs], cbuf.at[0], cs_sem.at[0], cr_sem.at[0], cpeer)]
-    p[0, mine] = dot(iht[mine], dz)
-    remote(tin, tin, ts_sem, tr_sem, opeer).wait_recv()
-    own = rows_at(xl * ROWS, ROWS)
-    dz = ((tout[own] + tin[...]) * tlen[own]).astype(BF16)
+    dz = edge_dz(total[:ROWS], across(total[ROWS:ROWS + 1]), tdir, tlen)
     p[1, theirs] = dot(tht[theirs], dz)
     ccopies.append(send(p.at[1, theirs], cbuf.at[1], cs_sem.at[1], cr_sem.at[1], cpeer))
     p[1, mine] = dot(tht[mine], dz)
@@ -320,18 +337,19 @@
         in_specs=[hbm] * 8,
         out_specs=pl.BlockSpec(memory_space=pltpu.VMEM),
         scratch_shapes=[
-            bf16(ROWS, D), bf16(ROWS, BLK), bf16(TXT, D), bf16(TXT, BLK), bf16(2, BLK, EDGE),
+            bf16(ROWS, D), bf16(ROWS, BLK), bf16(ROWS, D), bf16(ROWS, BLK), bf16(2, BLK, EDGE),
             f32(BLK, BLK), f32(EDGE, EDGE), f32(BLK, EDGE),
+            bf16(TXT, D), f32(ROWS, EDGE), f32(ROWS, EDGE),
             bf16(ROWS, D), f32(ROWS, EDGE), f32(ROWS, EDGE),
-            bf16(TXT, D), f32(TXT, EDGE), f32(TXT, EDGE),
             bf16(2, ROWS, D), f32(3, ROWS + 8, EDGE), f32(2, ROWS + 8, EDGE),
-            f32(TXT, EDGE), f32(ROWS, EDGE), bf16(BLK, ROWS), bf16(BLK, ROWS),
+            f32(TXT, EDGE), f32(TXT, EDGE), f32(ROWS + 8, EDGE), f32(ROWS + 8, EDGE),
+            bf16(BLK, ROWS), bf16(BLK, ROWS),
             bf16(BLK, BLK), bf16(BLK, BLK),
             f32(2, BLK, EDGE), f32(2, 512, EDGE), f32(2, NY, 2, 32, EDGE),
             bf16(3, NY, 32, EDGE), bf16(3, NY, 32, EDGE), f32(NY, 32, EDGE),
             bf16(NY, 32, EDGE), bf16(NY - 1, 32, EDGE), bf16(NZ, 32, EDGE),
             bf16(2 * NY, 2, 32, EDGE), f32(BLK, EDGE), pltpu.SemaphoreType.REGULAR,
-            dma((9,)), dma((2,)), dma((2,)), dma((2,)), dma((2,)), dma, dma,
+            dma((9,)), dma, dma, dma((2,)), dma((2,)), dma((2,)), dma((2,)), dma, dma,
             dma((2,)), dma((2,)), dma((3,)), dma((3,)), dma((NY - 1,)), dma((NY - 1,)),
             dma((NZ - 1,)), dma((NZ - 1,)), dma((2 * NY - 1,)), dma((2 * NY - 1,)),
             dma, dma,

time: 64.5 us -> 61.8 us (0.958)
  Pallas kernels: 61.9 us -> 59.7 us
    pallas_call x1, Pallas kernels: 61.9 us -> 59.7 us  [on_device(): pl.pallas_call(kernel, out_shape=jax.ShapeDtypeStruct((BLK, EDGE), F32),...]
where the time goes in v5:
time: 61.8 us; the launch traced here: 61.6 us
  Pallas kernels  59.7 us (97%)
  local copies, waits for them, and re-layouts  1.87 us (3%)
    pallas_call x1, Pallas kernels, on_device(): pl.pallas_call(kernel, out_shape=jax.ShapeDtypeStruct((BLK, EDGE), F32),...  59.7 us
    unnamed x1, local copies, waits for them, and re-layouts  1.87 us

profile of v5, /device:TPU:1, one launch (start us, length us, event | category | flops | bytes accessed | tf_op | source)
XLA Modules:
  0.0 61.6 jit_solution(17639243105795274307)
XLA Ops:
  0.0 59.7 %shard_map.82 = f32[1024,128]{1,0:T(8,128)} custom-call(bf16[128,1152]{1,0:T(8,128)(2,1)} %img_resid.1, bf16[128,1024]{1,0:T(8,128)(2,1)} %img_hidden.1, bf16[256,1152]{1,0:T(8,128)(2,1)} %txt_resid.1, bf16[256,1024]{1,0:T(8,128)(2,1)} %txt_hidden.1, bf16[2,1024,128]{2,1,0:T(8,128)(2,1)} %edge_weight.1, f32[1024,1024]{1,0:T(8,128)} %bitcast.4, ...), custom_call_target="tpu_custom_call" | custom-call | tf_op jit(solution)/shard_map/pallas_call | solution.py:334
  59.8 1.9 %copy.10 = f32[1,1024,128]{2,1,0:T(8,128)} copy(f32[1,1024,128]{2,1,0:T(8,128)} %bitcast.5) | data formatting | bytes 1048576

commit v6 on v5

--- a/solution.py
+++ b/solution.py
@@ -31,7 +31,7 @@
     ir, ih, tr, th, ew, left, right, acc,
     emb, idir, ilen, temb, tdir, tlen, vis, back, back_in, iedge, iradial, tout, tin,
     iht, tht, lhi, llo,
-    p, cbuf, acc1, xsend, xbuf, acc2, ysend, ybuf, zbuf, gbuf, cond, ready,
+    p, csend, cbuf, acc1, xsend, xbuf, acc2, ysend, ybuf, zbuf, gbuf, cond, ready, go,
     load_sem, es_sem, er_sem, vs_sem, vr_sem, bs_sem, br_sem, ts_sem, tr_sem,
     cs_sem, cr_sem, xs_sem, xr_sem, ys_sem, yr_sem, zs_sem, zr_sem,
     gs_sem, gr_sem, ks_sem, kr_sem,
@@ -115,13 +115,17 @@
     embed(tr, th, ew.at[1], temb, tdir, tlen)
     pl.semaphore_wait(barrier, len(peers))
 
-    far_copy = remote(temb, vis.at[1], vs_sem.at[1], vr_sem.at[1], along(2))
+    far = [
+        remote(temb.at[part], vis.at[1, part], vs_sem.at[n + 1], vr_sem.at[n + 1], along(2))
+        for n, part in enumerate((pl.ds(0, 64), pl.ds(64, 64)))
+    ]
     near_copy = remote(temb, vis.at[0], vs_sem.at[0], vr_sem.at[0], cpeer)
     onward = remote(vis.at[1], vis.at[0], vs_sem.at[0], vr_sem.at[0], cpeer)
 
     @pl.when(core == 1)
     def _():
-        far_copy.start()
+        far[0].start()
+        far[1].start()
 
     @pl.when(core == 0)
     def _():
@@ -136,12 +140,19 @@
     embed(ir, ih, ew.at[0], emb.at[half_rows], idir, ilen)
     send(emb.at[half_rows], emb.at[half_rows], es_sem, er_sem, opeer)
 
-    @pl.when(core == 0)
-    def _():
-        far_copy.start()
-
     iht[...] = ih[...].T
     tht[...] = th[...].T
+
+    @pl.when(core == 1)
+    def _():
+        far[0].wait_send()
+        pl.semaphore_signal(go, inc=1, device_id=cpeer, device_id_type=MESH)
+
+    @pl.when(core == 0)
+    def _():
+        pl.semaphore_wait(go, 1)
+        far[0].start()
+        far[1].start()
 
     def pair(view, diagonal):
         texts = view[...]
@@ -161,7 +172,8 @@
 
     @pl.when(core == 1)
     def _():
-        far_copy.wait_recv()
+        far[0].wait_recv()
+        far[1].wait_recv()
         onward.start()
 
     remote(emb.at[other_rows], emb.at[other_rows], es_sem, er_sem, opeer).wait_recv()
@@ -177,7 +189,8 @@
         else:
             @pl.when(core == 0)
             def _():
-                far_copy.wait_recv()
+                far[0].wait_recv()
+                far[1].wait_recv()
 
         edge, radial, img_edge, img_radial = pair(vis.at[slot], False)
         back[slot, :ROWS] = edge
@@ -185,7 +198,7 @@
         send(back.at[slot], back_in.at[slot], bs_sem.at[slot], br_sem.at[slot], before[slot])
         iedge[...] = iedge[...] + img_edge
         iradial[...] = iradial[...] + img_radial
-    sent.append(far_copy)
+    sent.append(far[1])
     sent.append(near_copy)
     tout[:ROWS] = iedge[other_rows]
     tout[ROWS:] = iradial[other_rows].T[:8]
@@ -203,22 +216,22 @@
     remote(tin, tin, ts_sem, tr_sem, opeer).wait_recv()
     radial = iradial[half_rows] + across(tin[ROWS:ROWS + 1])
     dz = edge_dz(iedge[half_rows] + tin[:ROWS], radial, idir, ilen)
-    p[0, theirs] = dot(iht[theirs], dz)
-    ccopies = [send(p.at[0, theirs], cbuf.at[0], cs_sem.at[0], cr_sem.at[0], cpeer)]
-    p[0, mine] = dot(iht[mine], dz)
+    csend[0] = dot(iht[theirs], dz).astype(BF16)
+    ccopies = [send(csend.at[0], cbuf.at[0], cs_sem.at[0], cr_sem.at[0], cpeer)]
+    p[0] = dot(iht[mine], dz)
     for slot in range(2):
         remote(
             back.at[slot], back_in.at[slot], bs_sem.at[slot], br_sem.at[slot], cpeer
         ).wait_recv()
     total = back[2] + back_in[0] + back_in[1]
     dz = edge_dz(total[:ROWS], across(total[ROWS:ROWS + 1]), tdir, tlen)
-    p[1, theirs] = dot(tht[theirs], dz)
-    ccopies.append(send(p.at[1, theirs], cbuf.at[1], cs_sem.at[1], cr_sem.at[1], cpeer))
-    p[1, mine] = dot(tht[mine], dz)
+    csend[1] = dot(tht[theirs], dz).astype(BF16)
+    ccopies.append(send(csend.at[1], cbuf.at[1], cs_sem.at[1], cr_sem.at[1], cpeer))
+    p[1] = dot(tht[mine], dz)
 
     for t in range(2):
         ccopies[t].wait_recv()
-        acc1[t] = (p[t, mine] + cbuf[t]).reshape(NY, 2, 32, EDGE)
+        acc1[t] = (p[t] + cbuf[t].astype(F32)).reshape(NY, 2, 32, EDGE)
         for h in (1, 0):
             k = lax.rem(2 * h + t + 4 - x, 4)
             slot = lax.max(k - 1, 0)
@@ -319,6 +332,10 @@
     for c in sent:
         c.wait_send()
 
+    @pl.when(core == 0)
+    def _():
+        far[0].wait_send()
+
 
 def on_device(*args):
     dma = pltpu.SemaphoreType.DMA
@@ -345,11 +362,12 @@
             f32(TXT, EDGE), f32(TXT, EDGE), f32(ROWS + 8, EDGE), f32(ROWS + 8, EDGE),
             bf16(BLK, ROWS), bf16(BLK, ROWS),
             bf16(BLK, BLK), bf16(BLK, BLK),
-            f32(2, BLK, EDGE), f32(2, 512, EDGE), f32(2, NY, 2, 32, EDGE),
+            f32(2, 512, EDGE), bf16(2, 512, EDGE), bf16(2, 512, EDGE), f32(2, NY, 2, 32, EDGE),
             bf16(3, NY, 32, EDGE), bf16(3, NY, 32, EDGE), f32(NY, 32, EDGE),
             bf16(NY, 32, EDGE), bf16(NY - 1, 32, EDGE), bf16(NZ, 32, EDGE),
-            bf16(2 * NY, 2, 32, EDGE), f32(BLK, EDGE), pltpu.SemaphoreType.REGULAR,
-            dma((9,)), dma, dma, dma((2,)), dma((2,)), dma((2,)), dma((2,)), dma, dma,
+            bf16(2 * NY, 2, 32, EDGE), f32(BLK, EDGE),
+            pltpu.SemaphoreType.REGULAR, pltpu.SemaphoreType.REGULAR,
+            dma((9,)), dma, dma, dma((3,)), dma((3,)), dma((2,)), dma((2,)), dma, dma,
             dma((2,)), dma((2,)), dma((3,)), dma((3,)), dma((NY - 1,)), dma((NY - 1,)),
             dma((NZ - 1,)), dma((NZ - 1,)), dma((2 * NY - 1,)), dma((2 * NY - 1,)),
             dma, dma,

time: 61.8 us -> 61.7 us (level)
  no operation moved by 1% of the time
where the time goes in v6:
time: 61.7 us; the launch traced here: 61.5 us
  Pallas kernels  59.7 us (97%)
  local copies, waits for them, and re-layouts  1.87 us (3%)
    pallas_call x1, Pallas kernels, on_device(): pl.pallas_call(kernel, out_shape=jax.ShapeDtypeStruct((BLK, EDGE), F32),...  59.7 us
    unnamed x1, local copies, waits for them, and re-layouts  1.87 us

profile of v6, /device:TPU:1, one launch (start us, length us, event | category | flops | bytes accessed | tf_op | source)
XLA Modules:
  0.0 61.5 jit_solution(9131027776067794283)
XLA Ops:
  0.0 59.7 %shard_map.82 = f32[1024,128]{1,0:T(8,128)} custom-call(bf16[128,1152]{1,0:T(8,128)(2,1)} %img_resid.1, bf16[128,1024]{1,0:T(8,128)(2,1)} %img_hidden.1, bf16[256,1152]{1,0:T(8,128)(2,1)} %txt_resid.1, bf16[256,1024]{1,0:T(8,128)(2,1)} %txt_hidden.1, bf16[2,1024,128]{2,1,0:T(8,128)(2,1)} %edge_weight.1, f32[1024,1024]{1,0:T(8,128)} %bitcast.4, ...), custom_call_target="tpu_custom_call" | custom-call | tf_op jit(solution)/shard_map/pallas_call | solution.py:351
  59.7 1.9 %copy.10 = f32[1,1024,128]{2,1,0:T(8,128)} copy(f32[1,1024,128]{2,1,0:T(8,128)} %bitcast.5) | data formatting | bytes 1048576

commit v7 on v6

--- a/solution.py
+++ b/solution.py
@@ -31,7 +31,7 @@
     ir, ih, tr, th, ew, left, right, acc,
     emb, idir, ilen, temb, tdir, tlen, vis, back, back_in, iedge, iradial, tout, tin,
     iht, tht, lhi, llo,
-    p, csend, cbuf, acc1, xsend, xbuf, acc2, ysend, ybuf, zbuf, gbuf, cond, ready, go,
+    p, csend, cbuf, acc1, xsend, xbuf, ysend, ybuf, zbuf, gbuf, cond, ready, go,
     load_sem, es_sem, er_sem, vs_sem, vr_sem, bs_sem, br_sem, ts_sem, tr_sem,
     cs_sem, cr_sem, xs_sem, xr_sem, ys_sem, yr_sem, zs_sem, zr_sem,
     gs_sem, gr_sem, ks_sem, kr_sem,
@@ -229,6 +229,7 @@
     ccopies.append(send(csend.at[1], cbuf.at[1], cs_sem.at[1], cr_sem.at[1], cpeer))
     p[1] = dot(tht[mine], dz)
 
+    pieces = [lax.rem(y + k, NY) for k in YORDER + (0,)]
     for t in range(2):
         ccopies[t].wait_recv()
         acc1[t] = (p[t] + cbuf[t].astype(F32)).reshape(NY, 2, 32, EDGE)
@@ -239,10 +240,11 @@
             @pl.when(k > 0)
             def _():
                 xsend[slot] = acc1[t, :, h].astype(BF16)
-                remote(
-                    xsend.at[slot], xbuf.at[slot], xs_sem.at[slot], xr_sem.at[slot],
-                    at(xh=h, xl=t),
-                ).start()
+                for n, q in enumerate(pieces):
+                    remote(
+                        xsend.at[slot, q], xbuf.at[slot, q], xs_sem.at[slot, n],
+                        xr_sem.at[slot, n], at(xh=h, xl=t),
+                    ).start()
 
     loads[6].wait()
 
@@ -254,22 +256,23 @@
         lhi[r] = high
         llo[r] = (value - high.astype(F32)).astype(BF16)
 
-    total = acc1[xl, :, xh]
-    for k in range(3):
-        c = remote(xsend.at[k], xbuf.at[k], xs_sem.at[k], xr_sem.at[k], cpeer)
-        c.wait_recv()
-        sent.append(c)
-        total = total + xbuf[k].astype(F32)
-    acc2[...] = total
-    ysend[...] = total.astype(BF16)
     pl.semaphore_wait(ready, len(near))
     ycopies = []
-    for k in YORDER:
-        py, d = ypeer[k - 1]
-        ycopies.append(send(
-            ysend.at[py], ybuf.at[k - 1], ys_sem.at[k - 1], yr_sem.at[k - 1], d
-        ))
-    part = acc2[y]
+    for n, q in enumerate(pieces):
+        part = acc1[xl, q, xh]
+        for k in range(3):
+            c = remote(
+                xsend.at[k, q], xbuf.at[k, q], xs_sem.at[k, n], xr_sem.at[k, n], cpeer
+            )
+            c.wait_recv()
+            sent.append(c)
+            part = part + xbuf[k, q].astype(F32)
+        if n < NY - 1:
+            ysend[q] = part.astype(BF16)
+            k = YORDER[n]
+            ycopies.append(send(
+                ysend.at[q], ybuf.at[k - 1], ys_sem.at[k - 1], yr_sem.at[k - 1], ypeer[k - 1][1]
+            ))
     for c in ycopies:
         c.wait_recv()
     for k in range(NY - 1):
@@ -363,12 +366,12 @@
             bf16(BLK, ROWS), bf16(BLK, ROWS),
             bf16(BLK, BLK), bf16(BLK, BLK),
             f32(2, 512, EDGE), bf16(2, 512, EDGE), bf16(2, 512, EDGE), f32(2, NY, 2, 32, EDGE),
-            bf16(3, NY, 32, EDGE), bf16(3, NY, 32, EDGE), f32(NY, 32, EDGE),
+            bf16(3, NY, 32, EDGE), bf16(3, NY, 32, EDGE),
             bf16(NY, 32, EDGE), bf16(NY - 1, 32, EDGE), bf16(NZ, 32, EDGE),
             bf16(2 * NY, 2, 32, EDGE), f32(BLK, EDGE),
             pltpu.SemaphoreType.REGULAR, pltpu.SemaphoreType.REGULAR,
             dma((9,)), dma, dma, dma((3,)), dma((3,)), dma((2,)), dma((2,)), dma, dma,
-            dma((2,)), dma((2,)), dma((3,)), dma((3,)), dma((NY - 1,)), dma((NY - 1,)),
+            dma((2,)), dma((2,)), dma((3, NY)), dma((3, NY)), dma((NY - 1,)), dma((NY - 1,)),
             dma((NZ - 1,)), dma((NZ - 1,)), dma((2 * NY - 1,)), dma((2 * NY - 1,)),
             dma, dma,
         ],

time: 61.7 us -> 61.4 us (level)
  no operation moved by 1% of the time
where the time goes in v7:
time: 61.4 us; the launch traced here: 61.2 us
  Pallas kernels  59.3 us (97%)
  local copies, waits for them, and re-layouts  1.87 us (3%)
    pallas_call x1, Pallas kernels, on_device(): pl.pallas_call(kernel, out_shape=jax.ShapeDtypeStruct((BLK, EDGE), F32),...  59.3 us
    unnamed x1, local copies, waits for them, and re-layouts  1.87 us

profile of v7, /device:TPU:1, one launch (start us, length us, event | category | flops | bytes accessed | tf_op | source)
XLA Modules:
  0.0 61.2 jit_solution(13109383471142456436)
XLA Ops:
  0.0 59.3 %shard_map.82 = f32[1024,128]{1,0:T(8,128)} custom-call(bf16[128,1152]{1,0:T(8,128)(2,1)} %img_resid.1, bf16[128,1024]{1,0:T(8,128)(2,1)} %img_hidden.1, bf16[256,1152]{1,0:T(8,128)(2,1)} %txt_resid.1, bf16[256,1024]{1,0:T(8,128)(2,1)} %txt_hidden.1, bf16[2,1024,128]{2,1,0:T(8,128)(2,1)} %edge_weight.1, f32[1024,1024]{1,0:T(8,128)} %bitcast.4, ...), custom_call_target="tpu_custom_call" | custom-call | tf_op jit(solution)/shard_map/pallas_call | solution.py:354
  59.3 1.9 %copy.10 = f32[1,1024,128]{2,1,0:T(8,128)} copy(f32[1,1024,128]{2,1,0:T(8,128)} %bitcast.5) | data formatting | bytes 1048576

commit v8 on v7

--- a/solution.py
+++ b/solution.py
@@ -57,7 +57,7 @@
         (left_hbm, left), (right_hbm, right), (acc_hbm, acc),
     ]):
         loads.append(pltpu.make_async_copy(src, dst, load_sem.at[n]))
-    for c in loads[:6]:
+    for c in loads[:3]:
         c.start()
 
     x = xh * 2 + xl
@@ -78,10 +78,20 @@
     side = along(2 * core - 1)
 
     barrier = pltpu.get_barrier_semaphore()
-    near = [ypeer[k - 1][1] for k in (1, 2, 6, 7)] + [zpeer[k - 1][1] for k in (1, 2, 3, 9, 10, 11)]
-    peers = [along(2), before[1], side, cpeer] + [d for _, d in xpeer] + near
-    for d in peers:
-        pl.semaphore_signal(barrier, inc=1, device_id=d, device_id_type=MESH)
+    one = [xpeer[0][1], xpeer[2][1]] + [ypeer[k - 1][1] for k in (1, 7)] + [
+        zpeer[k - 1][1] for k in (1, 11)
+    ]
+    z_two = [zpeer[k - 1][1] for k in (2, 10)]
+    two = [ypeer[k - 1][1] for k in (2, 6)] + z_two
+    peers = [along(2), before[1], side, cpeer] + one
+
+    def tell(sem, devices):
+        for d in devices:
+            pl.semaphore_signal(sem, inc=1, device_id=d, device_id_type=MESH)
+
+    tell(barrier, peers)
+    for c in loads[3:6]:
+        c.start()
 
     def remote(src, dst, s, r, d):
         return pltpu.make_async_remote_copy(
@@ -131,8 +141,7 @@
     def _():
         near_copy.start()
 
-    for d in near:
-        pl.semaphore_signal(ready, inc=1, device_id=d, device_id_type=MESH)
+    tell(ready.at[0], one)
     for c in loads[6:]:
         c.start()
     for n in range(3, 6):
@@ -176,12 +185,17 @@
         far[1].wait_recv()
         onward.start()
 
+    pl.semaphore_wait(ready.at[0], len(one))
+    tell(ready.at[1], two)
     remote(emb.at[other_rows], emb.at[other_rows], es_sem, er_sem, opeer).wait_recv()
     own_edge, own_radial, img_edge, img_radial = pair(temb, True)
     back[2, :ROWS] = own_edge
     back[2, ROWS:] = jnp.broadcast_to(own_radial, (8, EDGE))
     iedge[...] = img_edge
     iradial[...] = img_radial
+
+    pl.semaphore_wait(ready.at[1], len(two))
+    tell(ready.at[2], z_two)
 
     for slot in range(2):
         if slot == 0:
@@ -256,7 +270,7 @@
         lhi[r] = high
         llo[r] = (value - high.astype(F32)).astype(BF16)
 
-    pl.semaphore_wait(ready, len(near))
+    pl.semaphore_wait(ready.at[2], len(z_two))
     ycopies = []
     for n, q in enumerate(pieces):
         part = acc1[xl, q, xh]
@@ -369,7 +383,7 @@
             bf16(3, NY, 32, EDGE), bf16(3, NY, 32, EDGE),
             bf16(NY, 32, EDGE), bf16(NY - 1, 32, EDGE), bf16(NZ, 32, EDGE),
             bf16(2 * NY, 2, 32, EDGE), f32(BLK, EDGE),
-            pltpu.SemaphoreType.REGULAR, pltpu.SemaphoreType.REGULAR,
+            pltpu.SemaphoreType.REGULAR((3,)), pltpu.SemaphoreType.REGULAR,
             dma((9,)), dma, dma, dma((3,)), dma((3,)), dma((2,)), dma((2,)), dma, dma,
             dma((2,)), dma((2,)), dma((3, NY)), dma((3, NY)), dma((NY - 1,)), dma((NY - 1,)),
             dma((NZ - 1,)), dma((NZ - 1,)), dma((2 * NY - 1,)), dma((2 * NY - 1,)),

time: 61.4 us -> 60.4 us (0.984)
  Pallas kernels: 59.3 us -> 58.3 us
    pallas_call x1, Pallas kernels: 59.3 us -> 58.3 us  [on_device(): pl.pallas_call(kernel, out_shape=jax.ShapeDtypeStruct((BLK, EDGE), F32),...]
where the time goes in v8:
time: 60.4 us; the launch traced here: 60.1 us
  Pallas kernels  58.3 us (97%)
  local copies, waits for them, and re-layouts  1.87 us (3%)
    pallas_call x1, Pallas kernels, on_device(): pl.pallas_call(kernel, out_shape=jax.ShapeDtypeStruct((BLK, EDGE), F32),...  58.3 us
    unnamed x1, local copies, waits for them, and re-layouts  1.87 us

profile of v8, /device:TPU:1, one launch (start us, length us, event | category | flops | bytes accessed | tf_op | source)
XLA Modules:
  0.0 60.1 jit_solution(10845330886619802598)
XLA Ops:
  0.0 58.3 %shard_map.82 = f32[1024,128]{1,0:T(8,128)} custom-call(bf16[128,1152]{1,0:T(8,128)(2,1)} %img_resid.1, bf16[128,1024]{1,0:T(8,128)(2,1)} %img_hidden.1, bf16[256,1152]{1,0:T(8,128)(2,1)} %txt_resid.1, bf16[256,1024]{1,0:T(8,128)(2,1)} %txt_hidden.1, bf16[2,1024,128]{2,1,0:T(8,128)(2,1)} %edge_weight.1, f32[1024,1024]{1,0:T(8,128)} %bitcast.4, ...), custom_call_target="tpu_custom_call" | custom-call | tf_op jit(solution)/shard_map/pallas_call | solution.py:368
  58.3 1.9 %copy.10 = f32[1,1024,128]{2,1,0:T(8,128)} copy(f32[1,1024,128]{2,1,0:T(8,128)} %bitcast.5) | data formatting | bytes 1048576

commit v9 on v8

--- a/solution.py
+++ b/solution.py
@@ -312,6 +312,14 @@
     for n, (k, h) in enumerate(offsets):
         d = at(y=lax.rem(y + k, NY), xh=lax.rem(xh + h, 2))
         send(own, own, gs_sem.at[n], gr_sem.at[n], d)
+    early = len(sent) - len(offsets)
+    for c in sent[:early]:
+        c.wait_send()
+
+    @pl.when(core == 0)
+    def _():
+        far[0].wait_send()
+
     for n, (k, h) in enumerate(offsets):
         came = gbuf.at[core * NY + lax.rem(y + NY - k, NY), lax.rem(xh + h, 2)]
         remote(came, came, gs_sem.at[n], gr_sem.at[n], cpeer).wait_recv()
@@ -346,12 +354,8 @@
     more, csum = half(oc, False)
     factor = jnp.sqrt(gsum + more) / jnp.sqrt(csum + 1e-06)
     out_ref[...] = cond[...] * factor
-    for c in sent:
+    for c in sent[early:]:
         c.wait_send()
-
-    @pl.when(core == 0)
-    def _():
-        far[0].wait_send()
 
 
 def on_device(*args):

time: 60.4 us -> 60.3 us (level)
  no operation moved by 1% of the time
where the time goes in v9:
time: 60.3 us; the launch traced here: 60.1 us
  Pallas kernels  58.2 us (97%)
  local copies, waits for them, and re-layouts  1.87 us (3%)
    pallas_call x1, Pallas kernels, on_device(): pl.pallas_call(kernel, out_shape=jax.ShapeDtypeStruct((BLK, EDGE), F32),...  58.2 us
    unnamed x1, local copies, waits for them, and re-layouts  1.87 us

profile of v9, /device:TPU:1, one launch (start us, length us, event | category | flops | bytes accessed | tf_op | source)
XLA Modules:
  0.0 60.1 jit_solution(14044314034994448571)
XLA Ops:
  0.0 58.2 %shard_map.82 = f32[1024,128]{1,0:T(8,128)} custom-call(bf16[128,1152]{1,0:T(8,128)(2,1)} %img_resid.1, bf16[128,1024]{1,0:T(8,128)(2,1)} %img_hidden.1, bf16[256,1152]{1,0:T(8,128)(2,1)} %txt_resid.1, bf16[256,1024]{1,0:T(8,128)(2,1)} %txt_hidden.1, bf16[2,1024,128]{2,1,0:T(8,128)(2,1)} %edge_weight.1, f32[1024,1024]{1,0:T(8,128)} %bitcast.4, ...), custom_call_target="tpu_custom_call" | custom-call | tf_op jit(solution)/shard_map/pallas_call | solution.py:372
  58.2 1.9 %copy.10 = f32[1,1024,128]{2,1,0:T(8,128)} copy(f32[1,1024,128]{2,1,0:T(8,128)} %bitcast.5) | data formatting | bytes 1048576
